TPU v7x, 32 devices: a whole 2x2x4 slice. The times are simulated.
32 devices in a mesh: ctx: 4 (over y, x), head: 8 (over z, core).
Axes of the slice: x: 2, y: 2, z: 4, core: 2. Of those that a mesh axis runs over, the one named last changes fastest.
Arguments:
- tokens: bfloat16 [2048, 8192], P('ctx'), may hold values from -6 to 6
- w_zx: bfloat16 [8192, 2, 8192], P('ctx', None, 'head'), may hold values from -0.0625 to 0.0625
- zx_scale: float32 [2, 8192], P(None, 'head'), may hold values from 0.5 to 2
- w_bc: bfloat16 [8192, 8, 512], P('ctx'), may hold values from -0.0625 to 0.0625
- bc_scale: float32 [8, 512], replicated, may hold values from 0.5 to 2
- w_dt: bfloat16 [8192, 128], P('ctx', 'head'), may hold values from -0.0625 to 0.0625
- conv_x: float32 [5, 8192], P(None, 'head'), may hold values from -3 to 3
- conv_bc: float32 [5, 8, 512], replicated, may hold values from -3 to 3
- tail_x: bfloat16 [3, 8192], P(None, 'head'), may hold values from -6 to 6
- tail_bc: bfloat16 [3, 8, 512], replicated, may hold values from -6 to 6
- head_params: float32 [3, 128], P(None, 'head'), may hold values from -12 to 2, as said below
- init_state: float32 [128, 64, 256], P('head'), may hold values from -1.5 to 1.5
- norm_gain: float32 [8192], P('head'), may hold values from 0.5 to 1.5
Outputs:
- mixed: bfloat16 [2048, 8192], P('ctx', 'head')
Inputs may be any that keep to these rules, and one draw needn't show every extreme that they name: `head_params`: row 0 lies in -3.5 to -2.5 and row 2 in 0.5 to 1.5.
All inputs are finite; a program needn't handle non-finite values.
Results may differ from a plain program's by a relative error of at most 0.0052.
Values may be sent and summed in bfloat16 or wider, within the bound.
No kernel may reach another device: no remote copies, remote signals or barrier semaphores. Data moves between devices by JAX's collectives and lax.ppermute only.
A program may use at most 256 MiB of HBM per device.

v0:
```python
import jax
import jax.numpy as jnp
from jax import lax
from jax.sharding import PartitionSpec as P

H = 128
P_SIZE = 64
N = 256
G = 8
K = 4


def passed_along(x, axis, by):
    length = lax.axis_size(axis)
    pairs = [(i, i + by) for i in range(length) if 0 <= i + by < length]
    return lax.ppermute(x, axis, pairs)


def prefix(part, axis, combine, identity):
    place = lax.axis_index(axis)
    gathered = jax.tree.map(lambda a: lax.all_gather(a, axis), part)
    state = jax.tree.map(lambda a, e: jnp.zeros_like(a) + jnp.asarray(e, a.dtype), part, identity)

    def one(lap, state):
        return combine(
            state, jax.tree.map(lambda a: lax.dynamic_index_in_dim(a, lap, 0, False), gathered)
        )

    return lax.fori_loop(0, place, one, state)


def conv_silu(values, before, taps):
    length = values.shape[0]
    padded = jnp.concatenate([before, values], 0).astype(jnp.float32)
    summed = taps[K]
    for tap_index in range(K):
        summed = summed + taps[tap_index] * padded[tap_index : tap_index + length]
    return jax.nn.silu(summed).astype(jnp.bfloat16)


def pick_group(values, group_index, axis_index):
    chosen = lax.dynamic_index_in_dim(values, group_index, axis_index, keepdims=False)
    return chosen


def body(
    tokens,
    w_zx,
    zx_scale,
    w_bc,
    bc_scale,
    w_dt,
    conv_x,
    conv_bc,
    tail_x,
    tail_bc,
    head_params,
    init_state,
    norm_gain,
):
    highest = lax.Precision.HIGHEST
    tok_rows = tokens.shape[0]
    local_heads = head_params.shape[1]
    channels = local_heads * P_SIZE
    per_group = H // G
    group_index = lax.axis_index("head") * local_heads // per_group
    bc_rows = pick_group(w_bc, group_index, 1)
    bc_scales = pick_group(bc_scale, group_index, 0)
    bc_taps = pick_group(conv_bc, group_index, 1)
    bc_tail = pick_group(tail_bc, group_index, 1)
    zx_rows = w_zx.reshape(w_zx.shape[0], 2 * channels)
    pieces = (
        lax.all_gather(zx_rows, "ctx", axis=0, tiled=True),
        lax.all_gather(bc_rows, "ctx", axis=0, tiled=True),
        lax.all_gather(w_dt, "ctx", axis=0, tiled=True),
    )
    zx_sum, bc_sum, step_sum = tuple(
        (jnp.dot(tokens, piece, preferred_element_type=jnp.float32) for piece in pieces)
    )
    zx_val = (zx_sum.reshape(tok_rows, 2, channels) * zx_scale).astype(jnp.bfloat16)
    gate = zx_val[:, 0]
    inner_in = zx_val[:, 1]
    bc_val = (bc_sum * bc_scales).astype(jnp.bfloat16)
    step_size = jax.nn.softplus(step_sum + head_params[0])
    edge = jnp.concatenate([inner_in[tok_rows - (K - 1) :], bc_val[tok_rows - (K - 1) :]], 1)
    arrived = passed_along(edge, "ctx", 1)
    previous = jnp.concatenate([tail_x, bc_tail], 1)
    arrived = jnp.where(lax.axis_index("ctx") == 0, previous, arrived)
    xconv = conv_silu(inner_in, arrived[:, :channels], conv_x)
    bconv = conv_silu(bc_val, arrived[:, channels:], bc_taps)
    b_part = bconv[:, :N]
    c_part = bconv[:, N:]
    x_heads = xconv.reshape(tok_rows, local_heads, P_SIZE).astype(jnp.float32)
    rate = -jnp.exp(head_params[1]) * step_size
    cumul = jnp.cumsum(rate, 0)
    cumul_t = cumul.T
    order = jnp.arange(tok_rows)
    lower = order[:, None] >= order[None, :]
    spread = cumul_t[:, :, None] - cumul_t[:, None, :]
    decay = jnp.where(lower[None], jnp.exp(jnp.minimum(spread, 0.0)), 0.0)
    scores = jnp.dot(c_part, b_part.T, preferred_element_type=jnp.float32)
    weights = decay * scores[None] * step_size.T[:, None, :]
    inner = jnp.einsum("hts,shp->thp", weights, x_heads, precision=highest)
    log_total = cumul[tok_rows - 1]
    fade = jnp.exp(log_total[None, :] - cumul) * step_size
    local_state = jnp.einsum(
        "sh,shp,sn->hpn", fade, x_heads, b_part.astype(jnp.float32), precision=highest
    )

    def combine(earlier, later):
        return (earlier[0] + later[0], jnp.exp(later[0])[:, None, None] * earlier[1] + later[1])

    before_log, before_state = prefix(
        (log_total, local_state),
        "ctx",
        combine,
        (jnp.zeros_like(log_total), jnp.zeros_like(local_state)),
    )
    incoming = jnp.exp(before_log)[:, None, None] * init_state + before_state
    carried = (
        jnp.einsum("tn,hpn->thp", c_part.astype(jnp.float32), incoming, precision=highest)
        * jnp.exp(cumul)[:, :, None]
    )
    y_val = inner + carried + head_params[2][None, :, None] * x_heads
    gated = y_val.reshape(tok_rows, channels) * jax.nn.silu(gate.astype(jnp.float32))
    squares = jnp.sum(gated * gated, axis=1)
    slot_hits = (jnp.arange(G) == group_index).astype(jnp.float32)
    placed = slot_hits[:, None] * squares[None, :]
    group_sums = lax.psum(placed, "head")
    totals = lax.dynamic_index_in_dim(group_sums, group_index, 0, keepdims=False)
    meansq = totals / (per_group * P_SIZE)
    mixed = gated * lax.rsqrt(meansq + 1e-05)[:, None] * norm_gain
    return mixed.astype(jnp.bfloat16)


def solution(mesh):
    return jax.shard_map(
        body,
        mesh=mesh,
        in_specs=(
            P("ctx", None),
            P("ctx", None, "head"),
            P(None, "head"),
            P("ctx", None, None),
            P(),
            P("ctx", "head"),
            P(None, "head"),
            P(),
            P(None, "head"),
            P(),
            P(None, "head"),
            P("head", None, None),
            P("head"),
        ),
        out_specs=P("ctx", "head"),
        check_vma=False,
    )
```

profile of v0, /device:TPU:0, one launch (start us, length us, event | category | flops | bytes accessed | tf_op | source)
XLA Modules:
  0.0 557.8 jit_solution(1520333198363107479)
XLA Ops:
  6.5 7.4 %constant_dynamic-slice_fusion.8 = bf16[2048,1,512]{2,1,0:T(2,128)(2,1)S(1)} fusion(bf16[2048,8,512]{2,1,0:T(8,128)(2,1)} %param.18, s32[]{:T(128)S(6)} %select_n.44), kind=kLoop, calls=%fused_computation.102 | loop fusion | bytes 4194308 | tf_op jit(solution)/shard_map/jit(dynamic_index_in_dim)/dynamic_slice | solution.py:42
  13.9 1.9 copy.37
  15.8 0.0 all-gather.9.cloned.1.call-update
  15.9 0.0 all-gather.7.cloned.1.call-start
  15.9 10.6 %copy.41 = bf16[256,8,2,1024]{3,1,2,0:T(8,128)(2,1)} copy(bf16[256,8,2,1024]{3,2,1,0:T(2,128)(2,1)} %bitcast.133) | data formatting | bytes 16777216
  26.5 0.0 all-gather.7.cloned.1.call-update
  26.6 0.0 all-gather.11.cloned.1.call-start
  26.7 0.7 copy-done.8
  27.4 13.3 %all_gather.20 = bf16[8192,16]{0,1:T(8,128)(2,1)S(1)} all-gather(bf16[2048,16]{0,1:T(8,128)(2,1)S(1)} %copy-done.8), channel_id=1, replica_groups=mesh['ctx'=4,'head'=8] {'ctx'}, dimensions={0}, use_global_device_ids=true | all-gather | bytes 327680 | tf_op jit(solution)/shard_map/all_gather | solution.py:75
  40.7 5.6 %convolution_add_fusion = f32[512,16]{0,1:T(8,128)S(1)} fusion(bf16[512,8192]{1,0:T(8,128)(2,1)} %param.15, bf16[8192,16]{0,1:T(8,128)(2,1)S(1)} %all_gather.20, f32[16]{0:T(128)S(1)} %get-tuple-element.75), kind=kOutput, calls=%fused_computation.48 | convolution fusion | flops 134225920 | bytes 8683584 | tf_op jit(solution)/shard_map/dot_general | solution.py:78
  46.4 0.1 compare_select_fusion.1
  46.5 1.1 reduce-window.6
  47.6 0.2 slice_reduce_fusion
  47.8 0.7 constant_dynamic-slice_fusion.7
  48.5 0.8 constant_dynamic-slice_fusion.4
  49.3 0.1 copy_bitcast_fusion
  49.4 0.2 slice_reduce_fusion.1
  49.6 0.1 bitcast_exponential_fusion.1
  49.7 58.7 %all-gather.9.cloned.1.call-done = bf16[8192,1,512]{2,0,1:T(8,128)(2,1)} async-done(((bf16[2048,1,512]{2,0,1:T(8,128)(2,1)}), bf16[8192,1,512]{2,0,1:T(8,128)(2,1)}) %all-gather.9.cloned.1.call-update) | async-done | bytes 8388624 | tf_op jit(solution)/shard_map/all_gather | solution.py:74
  108.4 10.3 %fusion.37 = bf16[512,512]{1,0:T(8,128)(2,1)S(1)} fusion(bf16[512,8192]{1,0:T(8,128)(2,1)} %param.15, bf16[8192,1,512]{2,0,1:T(8,128)(2,1)} %all-gather.9.cloned.1.call-done, f32[512]{0:T(512)S(1)} %bitcast.155), kind=kOutput, calls=%fused_computation.47 | convolution fusion | flops 4295491584 | bytes 17303552 | tf_op jit(solution)/shard_map/dot_general | solution.py:78
  118.7 0.8 copy-done.7
  119.5 288.0 %all-gather.7.cloned.1.call-done = bf16[8192,2048]{1,0:T(8,128)(2,1)} async-done(((bf16[2048,2048]{1,0:T(8,128)(2,1)}), bf16[8192,2048]{1,0:T(8,128)(2,1)}) %all-gather.7.cloned.1.call-update) | async-done | bytes 33554448 | tf_op jit(solution)/shard_map/all_gather | solution.py:73
  407.5 23.8 %fusion.67 = f32[512,2048]{1,0:T(8,128)S(1)} fusion(bf16[512,8192]{1,0:T(8,128)(2,1)} %param.15, bf16[8192,2048]{1,0:T(8,128)(2,1)} %all-gather.7.cloned.1.call-done), kind=kOutput, calls=%fused_computation.115 | convolution fusion | flops 17179869184 | bytes 46137344 | tf_op jit(solution)/shard_map/dot_general | solution.py:78
  431.3 0.6 fusion.15
  432.0 3.6 collective-permute-start
  435.6 1.7 slice_convert_fusion
  437.3 0.3 maximum_convert_fusion
  437.6 1.3 multiply_convert_fusion
  438.9 1.3 copy.31
  440.2 1.2 maximum_convert_fusion.1
  441.5 0.7 multiply_convert_fusion.1
  442.1 0.5 copy-done.3
  442.7 2.3 fusion.16
  444.9 0.0 all-gather.11.cloned.1.call-update
  444.9 9.1 %all-gather.2 = f32[4,1,16]{2,1,0:T(1,128)S(1)} all-gather(f32[1,1,16]{2,1,0:T(1,128)S(1)} %bitcast.154), channel_id=1, replica_groups=mesh['ctx'=4,'head'=8] {'ctx'}, dimensions={0}, use_global_device_ids=true | all-gather | bytes 320 | tf_op jit(solution)/shard_map/all_gather | solution.py:21
  454.1 0.1 iota_compare_fusion
  454.1 3.0 copy.35
  457.1 1.3 fusion.52
  458.5 40.6 %all-gather.11.cloned.1.call-done = f32[64,64,256]{2,1,0:T(8,128)} async-done(((f32[16,64,256]{2,1,0:T(8,128)}), f32[64,64,256]{2,1,0:T(8,128)}) %all-gather.11.cloned.1.call-update) | async-done | bytes 4194320 | tf_op jit(solution)/shard_map/all_gather | solution.py:21
  499.0 0.1 broadcast_in_dim.9
  499.1 0.3 while.12
  499.5 2.5 fusion.44
  502.0 0.0 copy-done.6
  502.0 14.4 %multiply_reduce_fusion = (f32[512]{0:T(512)S(1)}, f32[512,16,64]{0,2,1:T(8,128)}) fusion(f32[512,16,64]{0,2,1:T(8,128)S(1)} %bitcast.138, bf16[512,16,64]{0,2,1:T(8,128)(2,1)S(1)} %bitcast.137, f32[16]{0:T(128)S(1)} %get-tuple-element.73, f32[512,16,64]{0,2,1:T(8,128)S(1)} %fusion.44, f32[512,16]{0,1:T(8,128)S(1)} %get-tuple-element.62, ...), kind=kOutput, calls=%fused_computation.42 | convolution fusion | flops 3248487936 | bytes 8751168 | tf_op jit(solution)/shard_map/hts,shp->thp/dot_general | solution.py:103
  516.4 2.9 copy.34
  519.3 0.1 broadcast_multiply_fusion
  519.4 28.5 %psum.7 = f32[8,512]{1,0:T(8,128)S(1)} all-reduce(f32[8,512]{1,0:T(8,128)S(1)} %broadcast_multiply_fusion), channel_id=1, replica_groups=mesh['ctx'=4,'head'=8] {'head'}, use_global_device_ids=true, to_apply=%region_5.6 | all-reduce | flops 4096 | bytes 32768 | tf_op jit(solution)/shard_map/psum | solution.py:129
  547.9 3.3 fusion.28
  (43 shorter events, 0.2 us)
Async XLA Ops:
  6.5 20.1 %copy-start = (bf16[3,8,512]{2,1,0:T(8,128)(2,1)S(1)}, bf16[3,8,512]{2,1,0:T(8,128)(2,1)}, u32[]{:S(2)}) copy-start(bf16[3,8,512]{2,1,0:T(8,128)(2,1)} %param.24) | copy-start | bytes 73732
  6.5 101.9 %all-gather.9.cloned.1.call-start = ((), (), s32[]{:S(2)}) async-start(), calls=%async_computation.1 | async-start | bytes 10485760 | tf_op jit(solution)/shard_map/all_gather | solution.py:74
  15.9 391.7 %all-gather.7.cloned.1.call-start = ((), (), s32[]{:S(2)}) async-start(), calls=%async_computation | async-start | bytes 41943040 | tf_op jit(solution)/shard_map/all_gather | solution.py:73
  26.5 0.9 copy-start.8
  26.5 14.1 %copy-start.13 = (f32[3,16]{1,0:T(4,128)S(1)}, f32[3,16]{1,0:T(4,128)}, u32[]{:S(2)}) copy-start(f32[3,16]{1,0:T(4,128)} %param.25) | copy-start | bytes 580
  26.6 472.5 %all-gather.11.cloned.1.call-start = ((), (), s32[]{:S(2)}) async-start(), calls=%async_computation.2 | async-start | bytes 5242880 | tf_op jit(solution)/shard_map/all_gather | solution.py:21
  40.7 8.9 %copy-start.9 = (f32[5,1024]{1,0:T(8,128)S(1)}, f32[5,1024]{1,0:T(8,128)}, u32[]{:S(2)}) copy-start(f32[5,1024]{1,0:T(8,128)} %param.21) | copy-start | bytes 61444
  118.7 0.8 copy-start.7
  119.5 311.8 %copy-start.10 = (f32[2,1024]{1,0:T(2,128)S(1)}, f32[2,1024]{1,0:T(2,128)}, u32[]{:S(2)}) copy-start(f32[2,1024]{1,0:T(2,128)} %param.17) | copy-start | bytes 24580
  432.0 5.3 copy-start.11
  432.0 5.3 collective-permute-start
  441.4 1.2 copy-start.3
  442.1 15.0 %copy-start.2 = (bf16[512,512]{1,0:T(8,128)(2,1)}, bf16[512,512]{1,0:T(8,128)(2,1)S(1)}, u32[]{:S(2)}) copy-start(bf16[512,512]{1,0:T(8,128)(2,1)S(1)} %multiply_convert_fusion.1) | copy-start | bytes 1572868
  499.4 2.5 copy-start.4
  499.4 2.5 copy-start.5
  499.5 2.5 copy-start.6
  516.4 31.6 %copy-start.12 = (f32[1024]{0:T(1024)S(1)}, f32[1024]{0:T(1024)}, u32[]{:S(2)}) copy-start(f32[1024]{0:T(1024)} %param.27) | copy-start | bytes 12292
  547.9 3.3 copy-start.1
Sparse Core Ops, SparseCore 0:
  16.0 92.4 all-gather.8
  110.3 297.2 all-gather.6
  445.1 53.9 all-gather.10
where the time goes:
time: 561 us; the launch traced here: 558 us
  waiting for transfers between devices  387 us (69%)
  matrix products  60.1 us (11%)
  blocking collectives  50.9 us (9%)
  local copies, waits for them, and re-layouts  31.3 us (6%)
  between operations  13.4 us (2%)
  other arithmetic  10.7 us (2%)
    all_gather x1, waiting for transfers between devices, body(): lax.all_gather(zx_rows, 'ctx', axis=0, tiled=True)  288 us
    all_gather x1, waiting for transfers between devices, body(): lax.all_gather(bc_rows, 'ctx', axis=0, tiled=True)  58.7 us
    all_gather x1, waiting for transfers between devices, prefix(): gathered = jax.tree.map(lambda a: lax.all_gather(a, axis), part)  40.6 us
    dot_general x3, matrix products, body(): jnp.dot(tokens, piece, preferred_element_type=jnp.float32)  39.7 us
    psum x1, blocking collectives, body(): group_sums = lax.psum(placed, 'head')  28.5 us
    unnamed x31, local copies, waits for them, and re-layouts  14.6 us
    dot_general x1, matrix products, body(): inner = jnp.einsum('hts,shp->thp', weights, x_heads, precision=highest)  14.4 us
    all_gather x1, blocking collectives, body(): lax.all_gather(w_dt, 'ctx', axis=0, tiled=True)  13.3 us
  transfers between devices with their start and end apart: 4, of which 3 were waited for; matrix products, arithmetic and copies ran while one was open for 6% of the time, Pallas kernels for 0%

commit v1 on v0

v1 whole, which is shorter than its diff:
```python
import functools
import jax
import jax.numpy as jnp
from jax import lax
from jax.experimental import pallas as pl
from jax.experimental.pallas import tpu as pltpu
from jax.sharding import PartitionSpec as P

H = 128
P_SIZE = 64
N = 256
G = 8
K = 4
SLOTS = 4
LANES = 128
EDGE = 8
TILE = 512
MIB = 1 << 20
BF16 = jnp.bfloat16
F32 = jnp.float32
VMEM = pl.BlockSpec(memory_space=pltpu.VMEM)
SMEM = pl.BlockSpec(memory_space=pltpu.SMEM)
ANY = pl.BlockSpec(memory_space=pl.ANY)


def shape_of(shape, dtype):
    return jax.ShapeDtypeStruct(shape, dtype)


def params(mib):
    return pltpu.CompilerParams(vmem_limit_bytes=mib * MIB)


def passed_along(x, axis, by):
    length = lax.axis_size(axis)
    pairs = [(i, i + by) for i in range(length) if 0 <= i + by < length]
    return lax.ppermute(x, axis, pairs)


def swapped(x, axis, by):
    length = lax.axis_size(axis)
    return lax.ppermute(x, axis, [(i, i ^ by) for i in range(length)])


def pick_group(values, group_index, axis_index):
    return lax.dynamic_index_in_dim(values, group_index, axis_index, keepdims=False)


def dot32(a, b):
    return jnp.dot(a, b, preferred_element_type=F32)


def silu(v):
    return v / (1.0 + jnp.exp(-v))


def sent_kernel(count, main_tiles, *refs):
    rows, (w_ref, side_ref), out_ref = refs[:count], refs[count : count + 2], refs[-1]
    tile = pl.program_id(0)

    def product(weights):
        x = jnp.concatenate([r[...] for r in rows], 0)
        out_ref[...] = dot32(x, weights[...]).astype(BF16)

    pl.when(tile < main_tiles)(lambda: product(w_ref))
    pl.when(tile >= main_tiles)(lambda: product(side_ref))


def weight_specs(depth, first_tile, main_tiles):
    return [
        pl.BlockSpec((depth, TILE), lambda i, *_: (0, first_tile + jnp.minimum(i, main_tiles - 1))),
        pl.BlockSpec((depth, TILE), lambda i, *_: (0, 0)),
    ]


def sent_product(rows, w_all, side, first_tile, tiles, after):
    depth = w_all.shape[0]
    part = rows[0].shape[0]
    main_tiles = tiles[0]
    total = sum(tiles)
    return pl.pallas_call(
        functools.partial(sent_kernel, len(rows), main_tiles),
        grid=(total,),
        in_specs=[pl.BlockSpec((part, depth), lambda i: (0, 0))] * len(rows)
        + weight_specs(depth, first_tile, main_tiles)
        + [ANY] * len(after),
        out_specs=pl.BlockSpec((part * len(rows), TILE), lambda i: (0, i)),
        out_shape=shape_of((part * len(rows), TILE * total), BF16),
        compiler_params=params(32),
    )(*rows, w_all, side, *after)


def kept_kernel(count, main_tiles, stay, gone, place_ref, *refs):
    rows, (w_ref, side_ref, got_ref) = refs[:count], refs[count : count + 3]
    stay_ref, gone_ref = refs[-2:]
    tile = pl.program_id(0)
    part = rows[0].shape[0]

    def product(weights):
        x = jnp.concatenate([r[...] for r in rows], 0)
        total = dot32(x, weights[...]) + got_ref[...].astype(F32)
        for to, i in enumerate(stay):
            stay_ref[to * part : (to + 1) * part] = total[i * part : (i + 1) * part]
        for to, i in enumerate(gone):
            gone_ref[to * part : (to + 1) * part] = total[i * part : (i + 1) * part].astype(BF16)

    pl.when(tile < main_tiles)(lambda: product(w_ref))
    pl.when(tile >= main_tiles)(lambda: product(side_ref))


def kept_product(place, tokens, rows, w_all, side, got, first_tile, tiles, stay, gone):
    depth = w_all.shape[0]
    part = tokens.shape[0] // SLOTS
    main_tiles = tiles[0]
    total = sum(tiles)
    count = len(rows) + 1
    return pl.pallas_call(
        functools.partial(kept_kernel, count, main_tiles, stay, gone),
        grid_spec=pltpu.PrefetchScalarGridSpec(
            num_scalar_prefetch=1,
            grid=(total,),
            in_specs=[pl.BlockSpec((part, depth), lambda i, place: (place[0], place[1]))]
            + [pl.BlockSpec((part, depth), lambda i, place: (0, 0))] * len(rows)
            + weight_specs(depth, first_tile, main_tiles)
            + [pl.BlockSpec((part * count, TILE), lambda i, place: (0, i))],
            out_specs=[
                pl.BlockSpec((part * len(stay), TILE), lambda i, place: (0, i)),
                pl.BlockSpec((part * len(gone), TILE), lambda i, place: (0, i)),
            ],
        ),
        out_shape=[
            shape_of((part * len(stay), TILE * total), F32),
            shape_of((part * len(gone), TILE * total), BF16),
        ],
        compiler_params=params(32),
    )(place, tokens, *rows, w_all, side, got)


class Reduction:
    def __init__(self, rows, bits, first_tile, tiles, w_all, side):
        self.rows, self.bits, self.first_tile, self.tiles = rows, bits, first_tile, tiles
        self.w_all, self.side = w_all, side
        self.n = len(rows) + 1

    def send(self, after=()):
        sent = [j for j in range(self.n) if j & self.bits[0]]
        self.sent = sent_product(
            [self.rows[j] for j in sent], self.w_all, self.side, self.first_tile, self.tiles, after
        )
        self.got = swapped(self.sent, "ctx", self.bits[0])

    def keep(self, place, tokens):
        kept = [j for j in range(self.n) if not j & self.bits[0]]
        bit = self.bits[1]
        gone = [i for i, j in enumerate(kept) if j & bit]
        stay = [i for i, j in enumerate(kept) if not j & bit]
        total, out = kept_product(
            place,
            tokens,
            [self.rows[j] for j in kept[1:]],
            self.w_all,
            self.side,
            self.got,
            self.first_tile,
            self.tiles,
            stay,
            gone,
        )
        self.kept = total
        kept = [kept[i] for i in stay]
        got = swapped(out, "ctx", bit)
        size = total.shape[0] // len(kept)
        for bit in self.bits[2:]:
            total = total + got.astype(F32)
            gone = [i for i, j in enumerate(kept) if j & bit]
            stay = [i for i, j in enumerate(kept) if not j & bit]
            parts = [total[i * size : (i + 1) * size] for i in range(len(kept))]
            out = jnp.concatenate([parts[i] for i in gone], 0).astype(BF16)
            total = jnp.concatenate([parts[i] for i in stay], 0)
            got = swapped(out, "ctx", bit)
            kept = [kept[i] for i in stay]
        self.total, self.last = total, got


def step_kernel(me_ref, tok_ref, w_ref, heads_ref, *refs):
    cum_t_ref, shift_t_ref, cum_ref, fade_ref, log_ref, acc = refs[-6:]
    j = pl.program_id(0)

    @pl.when(j == 0)
    def _():
        acc[...] = jnp.zeros_like(acc)

    acc[...] += lax.dot_general(
        w_ref[0], tok_ref[...], (((1,), (1,)), ((), ())), preferred_element_type=F32
    )

    @pl.when(j == pl.num_programs(0) - 1)
    def _():
        v = acc[...] + heads_ref[:, 0:1]
        step = jnp.maximum(v, 0.0) + jnp.log1p(jnp.exp(-jnp.abs(v)))
        rate = -jnp.exp(heads_ref[:, 1:2]) * step
        rows = rate.shape[1]
        up_to = lax.broadcasted_iota(jnp.int32, (rows, rows), 0) <= lax.broadcasted_iota(
            jnp.int32, (rows, rows), 1
        )
        cum = jnp.dot(
            rate, up_to.astype(F32), precision=lax.Precision.HIGHEST, preferred_element_type=F32
        )
        last = cum[:, rows - 1 : rows]
        cum_t_ref[...] = cum
        shift_t_ref[...] = cum - jnp.log(step)
        cum_ref[...] = cum.T
        fade_ref[...] = (jnp.exp(last - cum) * step).T
        log_ref[...] = jnp.broadcast_to(last, log_ref.shape)


def step_sizes(me, tokens, w_dt_all, heads, after):
    n, local_heads, depth = w_dt_all.shape
    rows = tokens.shape[0]
    return pl.pallas_call(
        step_kernel,
        grid_spec=pltpu.PrefetchScalarGridSpec(
            num_scalar_prefetch=1,
            grid=(n,),
            in_specs=[
                pl.BlockSpec((rows, depth), lambda j, me: (0, me[0] ^ j)),
                pl.BlockSpec((1, local_heads, depth), lambda j, me: (j, 0, 0)),
                pl.BlockSpec((local_heads, 3), lambda j, me: (0, 0)),
            ]
            + [ANY] * len(after),
            out_specs=[
                pl.BlockSpec((local_heads, rows), lambda j, me: (0, 0)),
                pl.BlockSpec((local_heads, rows), lambda j, me: (0, 0)),
                pl.BlockSpec((rows, local_heads), lambda j, me: (0, 0)),
                pl.BlockSpec((rows, local_heads), lambda j, me: (0, 0)),
                pl.BlockSpec((local_heads, LANES), lambda j, me: (0, 0)),
            ],
            scratch_shapes=[pltpu.VMEM((local_heads, rows), F32)],
        ),
        out_shape=[
            shape_of((local_heads, rows), F32),
            shape_of((local_heads, rows), F32),
            shape_of((rows, local_heads), F32),
            shape_of((rows, local_heads), F32),
            shape_of((local_heads, LANES), F32),
        ],
        compiler_params=params(32),
    )(me, tokens, w_dt_all, heads, *after)


def head_spread(local_heads):
    channels = local_heads * P_SIZE
    hit = (
        lax.broadcasted_iota(jnp.int32, (local_heads, channels), 1) // P_SIZE
        == lax.broadcasted_iota(jnp.int32, (local_heads, channels), 0)
    )
    return hit.astype(F32).astype(BF16)


def spread_heads(values, hits):
    high = values.astype(BF16)
    low = (values - high.astype(F32)).astype(BF16)
    return dot32(high, hits) + dot32(low, hits)


def conv_kernel(place_ref, *refs):
    totals, lasts = refs[:SLOTS], refs[SLOTS : 2 * SLOTS]
    edge_ref, scale_ref, taps_ref, fade_ref = refs[2 * SLOTS : 2 * SLOTS + 4]
    conv_ref, state_ref, vals = refs[-3:]
    part, width = totals[0].shape
    rows = part * SLOTS
    channels = width - 2 * N
    slot = place_ref[0]
    vals[:EDGE] = edge_ref[...]
    for k in range(SLOTS):
        start = pl.multiple_of(EDGE + (slot ^ k) * part, EDGE)
        whole = (totals[k][...] + lasts[k][...].astype(F32)) * scale_ref[...]
        vals[pl.ds(start, part)] = whole.astype(BF16).astype(F32)
    for c in range(0, width, 2 * LANES):
        cols = slice(c, c + 2 * LANES)
        for r in range(0, rows, part):
            summed = taps_ref[K : K + 1, cols]
            for tap in range(K):
                at = r + EDGE - (K - 1) + tap
                summed = summed + taps_ref[tap : tap + 1, cols] * vals[at : at + part, cols]
            conv_ref[r : r + part, cols] = silu(summed).astype(BF16)
    hits = head_spread(channels // P_SIZE)
    faded = spread_heads(fade_ref[...], hits) * conv_ref[:, :channels].astype(F32)
    state_ref[...] = lax.dot_general(
        conv_ref[:, channels : channels + N],
        faded.astype(BF16),
        (((0,), (0,)), ((), ())),
        preferred_element_type=F32,
    ).astype(BF16)


def conv_and_state(slot, totals, lasts, edge, scale, taps, fade):
    part, width = totals[0].shape
    rows = part * SLOTS
    return pl.pallas_call(
        conv_kernel,
        in_specs=[SMEM] + [VMEM] * (2 * SLOTS + 4),
        out_specs=[VMEM, VMEM],
        out_shape=[shape_of((rows, width), BF16), shape_of((N, width - 2 * N), BF16)],
        scratch_shapes=[pltpu.VMEM((rows + EDGE, width), F32)],
        compiler_params=params(40),
    )(slot, *totals, *lasts, edge, scale, taps, fade)


def inner_kernel(conv_ref, cum_ref, shift_t_ref, skip_ref, y_ref, scores):
    rows, width = conv_ref.shape
    channels = width - 2 * N
    size = LANES
    blocks = rows // size
    nt = (((1,), (1,)), ((), ()))
    scores[...] = lax.dot_general(
        conv_ref[:, channels + N :], conv_ref[:, channels : channels + N], nt, preferred_element_type=F32
    )
    lower = lax.broadcasted_iota(jnp.int32, (size, size), 0) >= lax.broadcasted_iota(
        jnp.int32, (size, size), 1
    )
    left = lax.broadcasted_iota(jnp.int32, (size, 2 * P_SIZE), 1) < P_SIZE
    for pair in range(channels // (2 * P_SIZE)):
        cols = slice(pair * 2 * P_SIZE, (pair + 1) * 2 * P_SIZE)
        for a in range(blocks):
            t = slice(a * size, (a + 1) * size)
            products = []
            for h in (2 * pair, 2 * pair + 1):
                here = cum_ref[t, h : h + 1]
                own = jnp.where(lower, here - shift_t_ref[h : h + 1, t], -jnp.inf)
                weights = jnp.exp(own) * scores[t, t]
                if a > 0:
                    before = slice(0, a * size)
                    earlier = jnp.exp(here - shift_t_ref[h : h + 1, before]) * scores[t, before]
                    weights = jnp.concatenate([earlier, weights], 1)
                products.append(dot32(weights.astype(BF16), conv_ref[: (a + 1) * size, cols]))
            y_ref[t, cols] = jnp.where(left, products[0], products[1]) + skip_ref[:, cols] * conv_ref[
                t, cols
            ].astype(F32)


def inner_output(conved, cum, shift_t, skip):
    rows, width = conved.shape
    channels = width - 2 * N
    return pl.pallas_call(
        inner_kernel,
        in_specs=[VMEM] * 4,
        out_specs=VMEM,
        out_shape=shape_of((rows, channels), F32),
        scratch_shapes=[pltpu.VMEM((rows, rows), F32)],
        compiler_params=params(32),
    )(conved, cum, shift_t, skip)


def final_kernel(whole_group, place_ref, *refs):
    totals, lasts = refs[:SLOTS], refs[SLOTS : 2 * SLOTS]
    y_ref, c_ref, state_ref, cum_ref, scale_ref, gain_ref = refs[2 * SLOTS : 2 * SLOTS + 6]
    outs = refs[2 * SLOTS + 6 :]
    part, channels = totals[0].shape
    slot = place_ref[0]
    hits = head_spread(channels // P_SIZE)
    for k in range(SLOTS):
        at = pl.ds(pl.multiple_of((slot ^ k) * part, part), part)
        carried = dot32(c_ref[at], state_ref[...])
        y = y_ref[at] + carried * spread_heads(jnp.exp(cum_ref[at]), hits)
        gate = ((totals[k][...] + lasts[k][...].astype(F32)) * scale_ref[...]).astype(BF16).astype(F32)
        gated = y * silu(gate)
        squares = jnp.sum(gated * gated, axis=1, keepdims=True)
        if whole_group:
            meansq = squares / (H // G * P_SIZE)
            outs[0][at] = (gated * lax.rsqrt(meansq + 1e-05) * gain_ref[...]).astype(BF16)
        else:
            outs[0][at] = gated
            outs[1][at] = jnp.broadcast_to(squares, (part, LANES))


def final_output(whole_group, slot, totals, lasts, y, c_part, state, cum, scale, gain):
    rows, channels = y.shape
    if whole_group:
        outs = [shape_of((rows, channels), BF16)]
    else:
        outs = [shape_of((rows, channels), F32), shape_of((rows, LANES), F32)]
    return pl.pallas_call(
        functools.partial(final_kernel, whole_group),
        in_specs=[SMEM] + [VMEM] * (2 * SLOTS + 6),
        out_specs=[VMEM] * len(outs),
        out_shape=outs,
        compiler_params=params(40),
    )(slot, *totals, *lasts, y, c_part, state, cum, scale, gain)


def body(
    tokens,
    w_zx,
    zx_scale,
    w_bc,
    bc_scale,
    w_dt,
    conv_x,
    conv_bc,
    tail_x,
    tail_bc,
    head_params,
    init_state,
    norm_gain,
):
    tok_rows = tokens.shape[0]
    depth = w_zx.shape[0]
    local_heads = head_params.shape[1]
    channels = local_heads * P_SIZE
    per_group = H // G
    n_ctx = lax.axis_size("ctx")
    me = lax.axis_index("ctx")
    head_place = lax.axis_index("head")
    group_index = head_place * local_heads // per_group
    bits = [1 << i for i in range(n_ctx.bit_length() - 1)]
    part = tok_rows // SLOTS
    slot = head_place % SLOTS
    slot_ref = slot[None].astype(jnp.int32)

    fetched = [None] + [
        swapped(lax.dynamic_slice(tokens, (slot * part, (me ^ j) * depth), (part, depth)), "ctx", j)
        for j in range(1, n_ctx)
    ]
    from_core = [None] + [swapped(a, "head", 1) for a in fetched[1:]]
    from_chip = [None] + [swapped(a, "head", 2) for a in fetched[1:]]
    from_both = [None] + [swapped(a, "head", 1) for a in from_chip[1:]]
    quarters = (fetched, from_core, from_chip, from_both)

    w_all = w_zx.reshape(depth, 2 * channels)
    bc_rows = pick_group(w_bc, group_index, 1)
    main = channels // TILE
    firsts, gates = [], []
    for k, rows in enumerate(quarters):
        order = bits if k in (0, 3) else bits[::-1]
        rows = dict(enumerate(rows))
        rows.pop(0)
        firsts.append(Reduction(rows, order, main, (main, 2 * N // TILE), w_all, bc_rows))
        gates.append(Reduction(rows, order, 0, (main, 0), w_all, bc_rows))
    places = [jnp.stack([slot ^ k, me]).astype(jnp.int32) for k in range(SLOTS)]
    firsts[0].send()
    firsts[1].send(after=(firsts[0].sent,))

    dt_t = w_dt.T
    w_dt_all = jnp.stack([dt_t] + [swapped(dt_t, "ctx", j) for j in range(1, n_ctx)])
    cum_t, shift_t, cum, fade, logs = step_sizes(
        me[None].astype(jnp.int32), tokens, w_dt_all, head_params.T, (firsts[1].sent,)
    )

    firsts[0].keep(places[0], tokens)
    gates[0].send(after=(firsts[0].kept,))
    firsts[1].keep(places[1], tokens)
    gates[1].send(after=(firsts[1].kept,))
    firsts[2].send(after=(firsts[0].kept,))
    firsts[3].send(after=(firsts[1].kept,))
    gates[0].keep(places[0], tokens)
    gates[1].keep(places[1], tokens)
    firsts[2].keep(places[2], tokens)
    firsts[3].keep(places[3], tokens)
    gates[2].send(after=(firsts[2].kept,))
    gates[3].send(after=(firsts[3].kept,))
    gates[2].keep(places[2], tokens)
    gates[3].keep(places[3], tokens)

    scale = jnp.concatenate([zx_scale[1], pick_group(bc_scale, group_index, 0)], 0)[None]
    taps = jnp.concatenate([conv_x, pick_group(conv_bc, group_index, 1)], 1)
    edge = jnp.zeros((K - 1, scale.shape[1]), F32)
    for k, one in enumerate(firsts):
        rows = one.total[part - (K - 1) :] + one.last[part - (K - 1) :].astype(F32)
        edge = jnp.where((slot ^ k) == SLOTS - 1, rows, edge)
    arrived = passed_along((edge * scale).astype(BF16), "ctx", 1)
    previous = jnp.concatenate([tail_x, pick_group(tail_bc, group_index, 1)], 1)
    arrived = jnp.where(me == 0, previous, arrived).astype(F32)
    arrived = jnp.concatenate([jnp.zeros((EDGE - (K - 1), arrived.shape[1]), F32), arrived], 0)
    conved, local_state = conv_and_state(
        slot_ref, [f.total for f in firsts], [f.last for f in firsts], arrived, scale, taps, fade
    )
    y_local = inner_output(conved, cum, shift_t, jnp.repeat(head_params[2], P_SIZE)[None])

    log_total = logs[:, 0]
    log_by = [log_total] + [swapped(log_total, "ctx", j) for j in range(1, n_ctx)]

    def fall(offsets, only_before):
        total = jnp.zeros_like(log_total)
        for j in offsets:
            total = total + (jnp.where((me ^ j) < me, log_by[j], 0.0) if only_before else log_by[j])
        return jnp.repeat(jnp.exp(total), P_SIZE)[None]

    init_t = init_state.reshape(channels, N).T
    incoming = fall(range(1, n_ctx), True) * init_t
    run = local_state
    for bit in bits:
        later = (me & bit) > 0
        if bit == bits[-1]:
            got = passed_along(run, "ctx", bit).astype(F32)
        else:
            got = swapped(run, "ctx", bit).astype(F32)
        incoming = incoming + jnp.where(later, fall(range(1, bit), True) * got, 0.0)
        if bit != bits[-1]:
            own_fall, got_fall = fall(range(bit), False), fall(range(bit, 2 * bit), False)
            run = jnp.where(
                later, own_fall * got + run.astype(F32), got_fall * run.astype(F32) + got
            ).astype(BF16)

    whole_group = local_heads >= per_group
    outs = final_output(
        whole_group,
        slot_ref,
        [g.total for g in gates],
        [g.last for g in gates],
        y_local,
        conved[:, channels + N :],
        incoming.astype(BF16),
        cum,
        zx_scale[0:1],
        norm_gain[None],
    )
    if whole_group:
        return outs[0]
    gated, squares = outs
    slot_hits = (jnp.arange(G) == group_index).astype(F32)
    group_sums = lax.psum(slot_hits[:, None] * squares[:, 0][None, :], "head")
    totals = lax.dynamic_index_in_dim(group_sums, group_index, 0, keepdims=False)
    meansq = totals / (per_group * P_SIZE)
    return (gated * lax.rsqrt(meansq + 1e-05)[:, None] * norm_gain).astype(BF16)


def solution(mesh):
    return jax.shard_map(
        body,
        mesh=mesh,
        in_specs=(
            P("ctx", None),
            P("ctx", None, "head"),
            P(None, "head"),
            P("ctx", None, None),
            P(),
            P("ctx", "head"),
            P(None, "head"),
            P(),
            P(None, "head"),
            P(),
            P(None, "head"),
            P("head", None, None),
            P("head"),
        ),
        out_specs=P("ctx", "head"),
        check_vma=False,
    )
```

time: 561 us -> 251 us (0.45)
  waiting for transfers between devices: 387 us -> 40.7 us
  Pallas kernels: 0 us -> 78.5 us
  matrix products: 60.1 us -> 0 us
  blocking collectives: 50.9 us -> 0 us
  local copies, waits for them, and re-layouts: 31.3 us -> 76.2 us
  starting transfers between devices: 3.68 us -> 41.7 us
  between operations: 13.4 us -> 0.96 us
    all_gather x3 -> x0, waiting for transfers between devices: 387 us -> none  [the longest x1 288 us: body(): lax.all_gather(zx_rows, 'ctx', axis=0, tiled=True)]
    pallas_call x0 -> x20, Pallas kernels: none -> 78.5 us  [the longest x8 31.5 us: kept_product(): pl.pallas_call(functools.partial(kept_kernel, count, main_tiles, stay, go...]
    dot_general x7 -> x0, matrix products: 60.1 us -> none  [the longest x3 39.7 us: body(): jnp.dot(tokens, piece, preferred_element_type=jnp.float32)]
    unnamed x31 -> x101, local copies, waits for them, and re-layouts: 14.6 us -> 59.7 us
    ppermute x0 -> x35, waiting for transfers between devices: none -> 40.7 us  [swapped(): return lax.ppermute(x, axis, [(i, i ^ by) for i in range(length)])]
    ppermute x0 -> x35, starting transfers between devices: none -> 35.2 us  [swapped(): return lax.ppermute(x, axis, [(i, i ^ by) for i in range(length)])]
    psum x1 -> x0, blocking collectives: 28.5 us -> none  [body(): group_sums = lax.psum(placed, 'head')]
    all_gather x2 -> x0, blocking collectives: 22.4 us -> none  [the longest x1 13.3 us: body(): lax.all_gather(w_dt, 'ctx', axis=0, tiled=True)]
  transfers between devices with their start and end apart: 4 -> 37, of which waited for: 3 -> 11; matrix products, arithmetic and copies ran while one was open for 6% -> 13% of each run, Pallas kernels for 0% -> 28%
where the time goes in v1:
time: 251 us; the launch traced here: 246 us
  Pallas kernels  78.5 us (31%)
  local copies, waits for them, and re-layouts  76.2 us (30%)
  starting transfers between devices  41.7 us (17%)
  waiting for transfers between devices  40.7 us (16%)
  other arithmetic  7.53 us (3%)
    unnamed x101, local copies, waits for them, and re-layouts  59.7 us
    ppermute x35, waiting for transfers between devices, swapped(): return lax.ppermute(x, axis, [(i, i ^ by) for i in range(length)])  40.7 us
    ppermute x35, starting transfers between devices, swapped(): return lax.ppermute(x, axis, [(i, i ^ by) for i in range(length)])  35.2 us
    pallas_call x8, Pallas kernels, kept_product(): pl.pallas_call(functools.partial(kept_kernel, count, main_tiles, stay, go...  31.5 us
    pallas_call x8, Pallas kernels, sent_product(): pl.pallas_call(functools.partial(sent_kernel, len(rows), main_tiles), gri...  28.7 us
    dynamic_slice x4, local copies, waits for them, and re-layouts, pick_group(): lax.dynamic_index_in_dim(values, group_index, axis_index, keepdims=False)  9.35 us
    pallas_call x1, Pallas kernels, conv_and_state(): pl.pallas_call(conv_kernel, in_specs=[SMEM] + [VMEM] * (2 * SLOTS + 4), o...  6.65 us
    ppermute x2, starting transfers between devices, passed_along(): return lax.ppermute(x, axis, pairs)  6.47 us
  transfers between devices with their start and end apart: 37, of which 11 were waited for; matrix products, arithmetic and copies ran while one was open for 13% of the time, Pallas kernels for 28%

profile of v1, /device:TPU:0, one launch (start us, length us, event | category | flops | bytes accessed | tf_op | source)
XLA Modules:
  0.0 245.6 jit_solution(15874634300798325713)
XLA Ops:
  0.0 2.6 %fusion.9 = (bf16[128,2048]{1,0:T(8,128)(2,1)}, bf16[128,2048]{1,0:T(8,128)(2,1)}, bf16[128,2048]{1,0:T(8,128)(2,1)}) fusion(bf16[512,8192]{1,0:T(8,128)(2,1)} %tok_ref.1, s32[]{:T(128)S(6)} %select_n.112, s32[]{:T(128)S(6)} %select_n.117, s32[]{:T(128)S(6)} %select_n.116, s32[]{:T(128)S(6)} %select_n.113), kind=kLoop, calls=%fused_computation.36 | loop fusion | bytes 3145744 | tf_op jit(solution)/shard_map/dynamic_slice | solution.py:422
  2.6 3.0 %collective-permute-start = (bf16[128,2048]{1,0:T(8,128)(2,1)}, bf16[128,2048]{1,0:T(8,128)(2,1)S(1)}, u32[]{:S(2)}, u32[]{:S(2)}) collective-permute-start(bf16[128,2048]{1,0:T(8,128)(2,1)} %get-tuple-element.51), channel_id=1, source_target_pairs={{0,16},{8,24},{16,0},{24,8},{1,17},{9,25},{17,1},{25,9},{2,18},{10... | collective-permute-start | bytes 1572872 | tf_op jit(solution)/shard_map/ppermute | solution.py:42
  7.0 10.3 %copy.23 = bf16[256,8,2,1024]{3,1,2,0:T(8,128)(2,1)} copy(bf16[256,8,2,1024]{3,2,1,0:T(2,128)(2,1)} %bitcast.67) | data formatting | bytes 16777216
  17.3 7.9 %constant_dynamic-slice_fusion.3 = bf16[2048,1,512]{2,1,0:T(2,128)(2,1)S(1)} fusion(bf16[2048,8,512]{2,1,0:T(8,128)(2,1)} %param.16, s32[]{:T(128)S(6)} %select_n.115), kind=kLoop, calls=%fused_computation.23 | loop fusion | bytes 4194308 | tf_op jit(solution)/shard_map/jit(dynamic_index_in_dim)/dynamic_slice | solution.py:46
  25.8 3.1 %collective-permute-done.refs_1_ = bf16[128,2048]{1,0:T(8,128)(2,1)S(1)} collective-permute-done((bf16[128,2048]{1,0:T(8,128)(2,1)}, bf16[128,2048]{1,0:T(8,128)(2,1)S(1)}, u32[]{:S(2)}, u32[]{:S(2)}) %collective-permute-start) | collective-permute-done | bytes 524320 | tf_op jit(solution)/shard_map/ppermute | solution.py:42
  30.3 3.5 %shard_map.127.refs_4_ = bf16[256,1536]{1,0:T(8,128)(2,1)S(1)} custom-call(bf16[128,2048]{1,0:T(8,128)(2,1)} %collective-permute-done.1.refs_0_, bf16[128,2048]{1,0:T(8,128)(2,1)S(1)} %collective-permute-done.2.refs_1_, bf16[2048,2048]{1,0:T(8,128)(2,1)S(1)} %bitcast.31, bf16[2048,512]{1,0:T(8,128)(2,1)S(1)} %bitcast.49), custom_call_target="tpu_custom_call" | custom-call | tf_op jit(solution)/shard_map/pallas_call | solution.py:81
  33.7 1.8 collective-permute-start.3
  37.5 3.3 %shard_map.131.refs_0_ = bf16[256,1536]{1,0:T(8,128)(2,1)} custom-call(bf16[128,2048]{1,0:T(8,128)(2,1)S(1)} %collective-permute-done.6.refs_0_, bf16[128,2048]{1,0:T(8,128)(2,1)S(1)} %collective-permute-done.7.refs_1_, bf16[2048,2048]{1,0:T(8,128)(2,1)S(1)} %bitcast.32, bf16[2048,512]{1,0:T(8,128)(2,1)S(1)} %bitcast.50, ...), custom_call_target="tpu_custom_call" | custom-call | tf_op jit(solution)/shard_map/pallas_call | solution.py:81
  43.9 6.8 %collective-permute-done.10.refs_1_ = bf16[128,2048]{1,0:T(8,128)(2,1)} collective-permute-done((bf16[128,2048]{1,0:T(8,128)(2,1)}, bf16[128,2048]{1,0:T(8,128)(2,1)}, u32[]{:S(2)}, u32[]{:S(2)}) %collective-permute-start.10) | collective-permute-done | bytes 524320 | tf_op jit(solution)/shard_map/ppermute | solution.py:42
  50.7 11.2 %collective-permute-done.12.refs_1_ = bf16[128,2048]{1,0:T(8,128)(2,1)} collective-permute-done((bf16[128,2048]{1,0:T(8,128)(2,1)S(1)}, bf16[128,2048]{1,0:T(8,128)(2,1)}, u32[]{:S(2)}, u32[]{:S(2)}) %collective-permute-start.12) | collective-permute-done | bytes 524320 | tf_op jit(solution)/shard_map/ppermute | solution.py:42
  63.5 3.4 %copy-done.3 = bf16[256,8,2,1024]{3,1,2,0:T(8,128)(2,1)S(1)} copy-done((bf16[256,8,2,1024]{3,1,2,0:T(8,128)(2,1)S(1)}, bf16[256,8,2,1024]{3,1,2,0:T(8,128)(2,1)}, u32[]{:S(2)}) %copy-start.3) | copy-done | bytes 8388632
  66.8 3.4 %copy-done.8 = bf16[512,8192]{1,0:T(8,128)(2,1)S(1)} copy-done((bf16[512,8192]{1,0:T(8,128)(2,1)S(1)}, bf16[512,8192]{1,0:T(8,128)(2,1)}, u32[]{:S(2)}) %copy-start.8) | copy-done | bytes 8388632
  71.4 3.3 %shard_map.128 = (f32[128,1536]{1,0:T(8,128)S(1)}, bf16[128,1536]{1,0:T(8,128)(2,1)S(1)}) custom-call(s32[2]{0:T(128)S(1)} %pad_add_fusion.place_ref, bf16[512,8192]{1,0:T(8,128)(2,1)S(1)} %copy-done.8, bf16[128,2048]{1,0:T(8,128)(2,1)S(1)} %collective-permute-done.refs_1_, bf16[2048,2048]{1,0:T(8,128)(2,1)S(1)} %bitcast.33, bf16[2048,512]{1,0:T(8,128)(2,1)S(1)} %bitcast.51, ...), custom_call_target="tpu_custom_call" | custom-call | tf_op jit(solution)/shard_map/pallas_call | solution.py:117
  74.7 4.3 %shard_map.135 = bf16[256,1536]{1,0:T(8,128)(2,1)} custom-call(bf16[128,2048]{1,0:T(8,128)(2,1)} %collective-permute-done.11.refs_0_, bf16[128,2048]{1,0:T(8,128)(2,1)} %collective-permute-done.12.refs_1_, bf16[2048,2048]{1,0:T(8,128)(2,1)S(1)} %bitcast.34, bf16[2048,512]{1,0:T(8,128)(2,1)S(1)} %bitcast.52, f32[128,1536]{1,0:T(8,128)S(1)} %get-tuple-element.27.refs_4_.refs_0_), custom_call_target="tpu_custom_call" | custom-call | tf_op jit(solution)/shard_map/pallas_call | solution.py:81
  80.5 3.4 %copy-done.9 = bf16[512,8192]{1,0:T(8,128)(2,1)S(1)} copy-done((bf16[512,8192]{1,0:T(8,128)(2,1)S(1)}, bf16[512,8192]{1,0:T(8,128)(2,1)}, u32[]{:S(2)}) %copy-start.9) | copy-done | bytes 8388632
  83.9 4.3 %shard_map.132 = (f32[128,1536]{1,0:T(8,128)S(1)}, bf16[128,1536]{1,0:T(8,128)(2,1)S(1)}) custom-call(s32[2]{0:T(128)S(1)} %pad_add_fusion.1.place_ref, bf16[512,8192]{1,0:T(8,128)(2,1)S(1)} %copy-done.9, bf16[128,2048]{1,0:T(8,128)(2,1)} %collective-permute-done.5.refs_1_, bf16[2048,2048]{1,0:T(8,128)(2,1)S(1)} %bitcast.35, bf16[2048,512]{1,0:T(8,128)(2,1)S(1)} %bitcast.53, ...), custom_call_target="tpu_custom_call" | custom-call | tf_op jit(solution)/shard_map/pallas_call | solution.py:117
  88.3 4.5 %shard_map.139 = bf16[256,1536]{1,0:T(8,128)(2,1)} custom-call(bf16[128,2048]{1,0:T(8,128)(2,1)} %collective-permute-done.16.refs_0_, bf16[128,2048]{1,0:T(8,128)(2,1)} %collective-permute-done.17.refs_1_, bf16[2048,2048]{1,0:T(8,128)(2,1)S(1)} %bitcast.36, bf16[2048,512]{1,0:T(8,128)(2,1)S(1)} %bitcast.54, f32[128,1536]{1,0:T(8,128)S(1)} %get-tuple-element.29.refs_4_.refs_1_), custom_call_target="tpu_custom_call" | custom-call | tf_op jit(solution)/shard_map/pallas_call | solution.py:81
  99.1 3.4 %copy-done.4 = bf16[256,8,2,1024]{3,1,2,0:T(8,128)(2,1)S(1)} copy-done((bf16[256,8,2,1024]{3,1,2,0:T(8,128)(2,1)S(1)}, bf16[256,8,2,1024]{3,1,2,0:T(8,128)(2,1)}, u32[]{:S(2)}) %copy-start.4) | copy-done | bytes 8388632
  102.5 3.4 %copy-done.10 = bf16[512,8192]{1,0:T(8,128)(2,1)S(1)} copy-done((bf16[512,8192]{1,0:T(8,128)(2,1)S(1)}, bf16[512,8192]{1,0:T(8,128)(2,1)}, u32[]{:S(2)}) %copy-start.10) | copy-done | bytes 8388632
  105.9 5.0 %shard_map.136 = (f32[128,1536]{1,0:T(8,128)S(1)}, bf16[128,1536]{1,0:T(8,128)(2,1)}) custom-call(s32[2]{0:T(128)S(1)} %pad_add_fusion.2.place_ref, bf16[512,8192]{1,0:T(8,128)(2,1)S(1)} %copy-done.10, bf16[128,2048]{1,0:T(8,128)(2,1)} %collective-permute-done.10.refs_1_, bf16[2048,2048]{1,0:T(8,128)(2,1)S(1)} %bitcast.37, bf16[2048,512]{1,0:T(8,128)(2,1)S(1)} %bitcast.55, ...), custom_call_target="tpu_custom_call" | custom-call | tf_op jit(solution)/shard_map/pallas_call | solution.py:117
  113.6 4.8 %shard_map.140 = (f32[128,1536]{1,0:T(8,128)S(1)}, bf16[128,1536]{1,0:T(8,128)(2,1)}) custom-call(s32[2]{0:T(128)S(1)} %pad_add_fusion.3.place_ref, bf16[512,8192]{1,0:T(8,128)(2,1)S(1)} %copy-done.10, bf16[128,2048]{1,0:T(8,128)(2,1)S(1)} %collective-permute-done.15.refs_1_, bf16[2048,2048]{1,0:T(8,128)(2,1)S(1)} %bitcast.38, ...), custom_call_target="tpu_custom_call" | custom-call | tf_op jit(solution)/shard_map/pallas_call | solution.py:117
  124.0 7.3 %collective-permute-done.26.refs_6_ = bf16[128,1536]{1,0:T(8,128)(2,1)} collective-permute-done((bf16[128,1536]{1,0:T(8,128)(2,1)}, bf16[128,1536]{1,0:T(8,128)(2,1)}, u32[]{:S(2)}, u32[]{:S(2)}) %collective-permute-start.26) | collective-permute-done | bytes 393248 | tf_op jit(solution)/shard_map/ppermute | solution.py:42
  132.2 2.4 collective-permute-start.28
  135.6 3.4 %copy-done.11 = bf16[512,8192]{1,0:T(8,128)(2,1)S(1)} copy-done((bf16[512,8192]{1,0:T(8,128)(2,1)S(1)}, bf16[512,8192]{1,0:T(8,128)(2,1)}, u32[]{:S(2)}) %copy-start.11) | copy-done | bytes 8388632
  139.0 4.8 %shard_map.143 = (f32[16,512]{1,0:T(8,128)}, f32[16,512]{1,0:T(8,128)S(1)}, f32[512,16]{1,0:T(8,128)S(1)}, f32[512,16]{1,0:T(8,128)S(1)}, f32[16,128]{1,0:T(8,128)S(1)}) custom-call(s32[1]{0:T(128)} %bitcast.1.me_ref, bf16[512,8192]{1,0:T(8,128)(2,1)S(1)} %copy-done.11, bf16[4,16,2048]{2,1,0:T(8,128)(2,1)S(1)} %pad_maximum_fusion.w_ref, ...), custom_call_target="tpu_custom_call" | custom-call | tf_op jit(solution)/shard_map/pallas_call | solution.py:220
  145.3 6.6 %shard_map.144 = (bf16[512,1536]{1,0:T(8,128)(2,1)S(1)}, bf16[256,1024]{1,0:T(8,128)(2,1)}) custom-call(s32[1]{0:T(128)} %bitcast.place_ref, f32[128,1536]{1,0:T(8,128)S(1)} %get-tuple-element.27.refs_4_.refs_0_, f32[128,1536]{1,0:T(8,128)S(1)} %copy-done.16, f32[128,1536]{1,0:T(8,128)S(1)} %copy-done.19, f32[128,1536]{1,0:T(8,128)S(1)} %copy-done.22, ...), custom_call_target="tpu_custom_call" | custom-call | tf_op jit(solution)/shard_map/pallas_call | solution.py:300
  158.3 6.4 %collective-permute-done.34 = f32[16]{0:T(128)S(1)} collective-permute-done((f32[16]{0:T(128)S(1)}, f32[16]{0:T(128)S(1)}, u32[]{:S(2)}, u32[]{:S(2)}) %collective-permute-start.34) | collective-permute-done | bytes 96 | tf_op jit(solution)/shard_map/ppermute | solution.py:42
  165.3 3.4 %copy-done.5 = bf16[256,8,2,1024]{3,1,2,0:T(8,128)(2,1)S(1)} copy-done((bf16[256,8,2,1024]{3,1,2,0:T(8,128)(2,1)S(1)}, bf16[256,8,2,1024]{3,1,2,0:T(8,128)(2,1)}, u32[]{:S(2)}) %copy-start.5) | copy-done | bytes 8388632
  169.7 3.5 %shard_map.129 = bf16[256,1024]{1,0:T(8,128)(2,1)} custom-call(bf16[128,2048]{1,0:T(8,128)(2,1)} %collective-permute-done.1.refs_0_, bf16[128,2048]{1,0:T(8,128)(2,1)S(1)} %copy-done.27, bf16[2048,2048]{1,0:T(8,128)(2,1)S(1)} %bitcast.39, bf16[2048,512]{1,0:T(8,128)(2,1)S(1)} %bitcast.57, f32[128,1536]{1,0:T(8,128)S(1)} %get-tuple-element.27.refs_4_.refs_0_), custom_call_target="tpu_custom_call" | custom-call | tf_op jit(solution)/shard_map/pallas_call | solution.py:81
  174.7 3.4 %copy-done.6 = bf16[256,8,2,1024]{3,1,2,0:T(8,128)(2,1)S(1)} copy-done((bf16[256,8,2,1024]{3,1,2,0:T(8,128)(2,1)S(1)}, bf16[256,8,2,1024]{3,1,2,0:T(8,128)(2,1)}, u32[]{:S(2)}) %copy-start.6) | copy-done | bytes 8388632
  178.1 2.5 %shard_map.133 = bf16[256,1024]{1,0:T(8,128)(2,1)} custom-call(bf16[128,2048]{1,0:T(8,128)(2,1)S(1)} %copy-done.31, bf16[128,2048]{1,0:T(8,128)(2,1)S(1)} %copy-done.33, bf16[2048,2048]{1,0:T(8,128)(2,1)S(1)} %bitcast.40, bf16[2048,512]{1,0:T(8,128)(2,1)S(1)} %bitcast.58, f32[128,1536]{1,0:T(8,128)S(1)} %copy-done.17), custom_call_target="tpu_custom_call" | custom-call | tf_op jit(solution)/shard_map/pallas_call | solution.py:81
  181.9 3.6 %shard_map.137 = bf16[256,1024]{1,0:T(8,128)(2,1)} custom-call(bf16[128,2048]{1,0:T(8,128)(2,1)} %collective-permute-done.11.refs_0_, bf16[128,2048]{1,0:T(8,128)(2,1)} %collective-permute-done.12.refs_1_, bf16[2048,2048]{1,0:T(8,128)(2,1)S(1)} %bitcast.41, bf16[2048,512]{1,0:T(8,128)(2,1)S(1)} %bitcast.59, f32[128,1536]{1,0:T(8,128)S(1)} %copy-done.20), custom_call_target="tpu_custom_call" | custom-call | tf_op jit(solution)/shard_map/pallas_call | solution.py:81
  186.1 3.6 %shard_map.141 = bf16[256,1024]{1,0:T(8,128)(2,1)} custom-call(bf16[128,2048]{1,0:T(8,128)(2,1)} %collective-permute-done.16.refs_0_, bf16[128,2048]{1,0:T(8,128)(2,1)} %collective-permute-done.17.refs_1_, bf16[2048,2048]{1,0:T(8,128)(2,1)S(1)} %bitcast.42, bf16[2048,512]{1,0:T(8,128)(2,1)S(1)} %bitcast.60, f32[128,1536]{1,0:T(8,128)S(1)} %copy-done.23), custom_call_target="tpu_custom_call" | custom-call | tf_op jit(solution)/shard_map/pallas_call | solution.py:81
  190.3 2.3 fusion.1
  192.6 4.0 %collective-permute-start.36 = (bf16[256,1024]{1,0:T(8,128)(2,1)}, bf16[256,1024]{1,0:T(8,128)(2,1)}, u32[]{:S(2)}, u32[]{:S(2)}) collective-permute-start(bf16[256,1024]{1,0:T(8,128)(2,1)} %fusion.1), channel_id=1, source_target_pairs={{0,16},{8,24},{1,17},{9,25},{2,18},{10,26},{3,19},{11,27},{4,20},{... | collective-permute-start | bytes 1572872 | tf_op jit(solution)/shard_map/ppermute | solution.py:37
  197.4 2.5 %copy.19 = f32[1024,256]{0,1:T(8,128)} copy(f32[1024,256]{1,0:T(8,128)} %bitcast.68) | data formatting | bytes 2097152 | tf_op jit(solution)/shard_map/reshape | solution.py:489
  200.8 3.4 %copy-done.7 = bf16[256,8,2,1024]{3,1,2,0:T(8,128)(2,1)S(1)} copy-done((bf16[256,8,2,1024]{3,1,2,0:T(8,128)(2,1)S(1)}, bf16[256,8,2,1024]{3,1,2,0:T(8,128)(2,1)}, u32[]{:S(2)}) %copy-start.7) | copy-done | bytes 8388632
  204.2 3.4 %copy-done.12 = bf16[512,8192]{1,0:T(8,128)(2,1)S(1)} copy-done((bf16[512,8192]{1,0:T(8,128)(2,1)S(1)}, bf16[512,8192]{1,0:T(8,128)(2,1)}, u32[]{:S(2)}) %copy-start.12) | copy-done | bytes 8388632
  207.6 4.1 %shard_map.130 = (f32[128,1024]{1,0:T(8,128)S(1)}, bf16[128,1024]{1,0:T(8,128)(2,1)}) custom-call(s32[2]{0:T(128)S(1)} %pad_add_fusion.place_ref, bf16[512,8192]{1,0:T(8,128)(2,1)S(1)} %copy-done.12, bf16[128,2048]{1,0:T(8,128)(2,1)S(1)} %collective-permute-done.refs_1_, bf16[2048,2048]{1,0:T(8,128)(2,1)S(1)} %bitcast.43, bf16[2048,512]{1,0:T(8,128)(2,1)S(1)} %bitcast.61, ...), custom_call_target="tpu_custom_call" | custom-call | tf_op jit(solution)/shard_map/pallas_call | solution.py:117
  211.7 4.0 %shard_map.134 = (f32[128,1024]{1,0:T(8,128)S(1)}, bf16[128,1024]{1,0:T(8,128)(2,1)}) custom-call(s32[2]{0:T(128)S(1)} %pad_add_fusion.1.place_ref, bf16[512,8192]{1,0:T(8,128)(2,1)S(1)} %copy-done.12, bf16[128,2048]{1,0:T(8,128)(2,1)} %collective-permute-done.5.refs_1_, bf16[2048,2048]{1,0:T(8,128)(2,1)S(1)} %bitcast.44, bf16[2048,512]{1,0:T(8,128)(2,1)S(1)} %bitcast.62, ...), custom_call_target="tpu_custom_call" | custom-call | tf_op jit(solution)/shard_map/pallas_call | solution.py:117
  217.2 4.0 %copy-done.13 = bf16[512,8192]{1,0:T(8,128)(2,1)S(1)} copy-done((bf16[512,8192]{1,0:T(8,128)(2,1)S(1)}, bf16[512,8192]{1,0:T(8,128)(2,1)}, u32[]{:S(2)}) %copy-start.13) | copy-done | bytes 8388632
  221.2 3.4 %shard_map.138 = (f32[128,1024]{1,0:T(8,128)S(1)}, bf16[128,1024]{1,0:T(8,128)(2,1)S(1)}) custom-call(s32[2]{0:T(128)S(1)} %pad_add_fusion.2.place_ref, bf16[512,8192]{1,0:T(8,128)(2,1)S(1)} %copy-done.13, bf16[128,2048]{1,0:T(8,128)(2,1)} %collective-permute-done.10.refs_1_, bf16[2048,2048]{1,0:T(8,128)(2,1)S(1)} %bitcast.45, ...), custom_call_target="tpu_custom_call" | custom-call | tf_op jit(solution)/shard_map/pallas_call | solution.py:117
  225.9 3.0 %shard_map.145.refs_8_ = f32[512,1024]{1,0:T(8,128)S(1)} custom-call(bf16[512,1536]{1,0:T(8,128)(2,1)S(1)} %copy-done.25, f32[512,16]{1,0:T(8,128)S(1)} %copy-done.35, f32[16,512]{1,0:T(8,128)S(1)} %get-tuple-element.46.shift_t_ref, f32[1,1024]{1,0:T(1,128)S(1)} %broadcast_in_dim_reshape.2.skip_ref), custom_call_target="tpu_custom_call" | custom-call | tf_op jit(solution)/shard_map/pallas_call | solution.py:345
  229.0 3.4 %copy-done.14 = bf16[512,8192]{1,0:T(8,128)(2,1)S(1)} copy-done((bf16[512,8192]{1,0:T(8,128)(2,1)S(1)}, bf16[512,8192]{1,0:T(8,128)(2,1)}, u32[]{:S(2)}) %copy-start.14) | copy-done | bytes 8388632
  232.4 2.5 %shard_map.142 = (f32[128,1024]{1,0:T(8,128)S(1)}, bf16[128,1024]{1,0:T(8,128)(2,1)S(1)}) custom-call(s32[2]{0:T(128)S(1)} %pad_add_fusion.3.place_ref, bf16[512,8192]{1,0:T(8,128)(2,1)S(1)} %copy-done.14, bf16[128,2048]{1,0:T(8,128)(2,1)S(1)} %copy-done.29, bf16[2048,2048]{1,0:T(8,128)(2,1)S(1)} %bitcast.48, bf16[2048,512]{1,0:T(8,128)(2,1)S(1)} %bitcast.64, ...), custom_call_target="tpu_custom_call" | custom-call | tf_op jit(solution)/shard_map/pallas_call | solution.py:117
  235.0 2.1 collective-permute-start.23
  238.6 2.8 %collective-permute-done.23.refs_7_ = bf16[128,1024]{1,0:T(8,128)(2,1)S(1)} collective-permute-done((bf16[128,1024]{1,0:T(8,128)(2,1)S(1)}, bf16[128,1024]{1,0:T(8,128)(2,1)S(1)}, u32[]{:S(2)}, u32[]{:S(2)}) %collective-permute-start.23) | collective-permute-done | bytes 262176 | tf_op jit(solution)/shard_map/ppermute | solution.py:42
  241.4 3.8 %shard_map.146 = bf16[512,1024]{1,0:T(8,128)(2,1)} custom-call(s32[1]{0:T(128)} %bitcast.place_ref, f32[128,1024]{1,0:T(8,128)S(1)} %get-tuple-element.28.refs_0_, f32[128,1024]{1,0:T(8,128)S(1)} %get-tuple-element.30.refs_1_, f32[128,1024]{1,0:T(8,128)S(1)} %get-tuple-element.32.refs_2_, f32[128,1024]{1,0:T(8,128)S(1)} %get-tuple-element.34.refs_3_, ...), custom_call_target="tpu_custom_call" | custom-call | tf_op jit(solution)/shard_map/pallas_call | solution.py:383
  (183 shorter events, 48.6 us)
Async XLA Ops:
  0.0 121.5 %copy-start = (f32[5,8,512]{2,1,0:T(8,128)S(1)}, f32[5,8,512]{2,1,0:T(8,128)}, u32[]{:S(2)}) copy-start(f32[5,8,512]{2,1,0:T(8,128)} %param.20) | copy-start | bytes 245764
  2.6 26.3 %collective-permute-start = (bf16[128,2048]{1,0:T(8,128)(2,1)}, bf16[128,2048]{1,0:T(8,128)(2,1)S(1)}, u32[]{:S(2)}, u32[]{:S(2)}) collective-permute-start(bf16[128,2048]{1,0:T(8,128)(2,1)} %get-tuple-element.51), channel_id=1, source_target_pairs={{0,16},{8,24},{16,0},{24,8},{1,17},{9,25},{17,1},{25,9},{2,18},{10... | collective-permute-start | bytes 1572872 | tf_op jit(solution)/shard_map/ppermute | solution.py:42
  5.5 23.4 %collective-permute-start.2 = (bf16[128,2048]{1,0:T(8,128)(2,1)}, bf16[128,2048]{1,0:T(8,128)(2,1)S(1)}, u32[]{:S(2)}, u32[]{:S(2)}) collective-permute-start(bf16[128,2048]{1,0:T(8,128)(2,1)} %get-tuple-element.49), channel_id=1, source_target_pairs={{0,24},{8,16},{16,8},{24,0},{1,25},{9,17},{17,9},{25,1},{2,26},{10... | collective-permute-start | bytes 1572872 | tf_op jit(solution)/shard_map/ppermute | solution.py:42
  7.0 23.3 %collective-permute-start.1 = (bf16[128,2048]{1,0:T(8,128)(2,1)}, bf16[128,2048]{1,0:T(8,128)(2,1)}, u32[]{:S(2)}, u32[]{:S(2)}) collective-permute-start(bf16[128,2048]{1,0:T(8,128)(2,1)} %get-tuple-element.50), channel_id=1, source_target_pairs={{0,8},{8,0},{16,24},{24,16},{1,9},{9,1},{17,25},{25,17},{2,10},{10... | collective-permute-start | bytes 1572872 | tf_op jit(solution)/shard_map/ppermute | solution.py:42
  17.3 13.0 %copy-start.2 = (bf16[256,8,2,1024]{3,1,2,0:T(8,128)(2,1)S(1)}, bf16[256,8,2,1024]{3,1,2,0:T(8,128)(2,1)}, u32[]{:S(2)}) copy-start(bf16[256,8,2,1024]{3,1,2,0:T(8,128)(2,1)} %copy.23) | copy-start | bytes 25165828
  28.9 8.6 %collective-permute-start.6 = (bf16[128,2048]{1,0:T(8,128)(2,1)S(1)}, bf16[128,2048]{1,0:T(8,128)(2,1)S(1)}, u32[]{:S(2)}, u32[]{:S(2)}) collective-permute-start(bf16[128,2048]{1,0:T(8,128)(2,1)S(1)} %collective-permute-done.refs_1_), channel_id=1, source_target_pairs={{0,1},{1,0},{2,3},{3,2},{4,5},{5,4},{6,7},{7,6},{8,9},{9,8},{10,11... | collective-permute-start | bytes 1572872 | tf_op jit(solution)/shard_map/ppermute | solution.py:42
  28.9 11.9 %copy-start.26 = (bf16[128,2048]{1,0:T(8,128)(2,1)}, bf16[128,2048]{1,0:T(8,128)(2,1)S(1)}, u32[]{:S(2)}) copy-start(bf16[128,2048]{1,0:T(8,128)(2,1)S(1)} %collective-permute-done.2.refs_1_) | copy-start | bytes 1572868
  28.9 8.6 %collective-permute-start.7 = (bf16[128,2048]{1,0:T(8,128)(2,1)S(1)}, bf16[128,2048]{1,0:T(8,128)(2,1)S(1)}, u32[]{:S(2)}, u32[]{:S(2)}) collective-permute-start(bf16[128,2048]{1,0:T(8,128)(2,1)S(1)} %collective-permute-done.2.refs_1_), channel_id=1, source_target_pairs={{0,1},{1,0},{2,3},{3,2},{4,5},{5,4},{6,7},{7,6},{8,9},{9,8},{10,11... | collective-permute-start | bytes 1572872 | tf_op jit(solution)/shard_map/ppermute | solution.py:42
  33.7 28.2 %collective-permute-start.3 = (bf16[256,1536]{1,0:T(8,128)(2,1)S(1)}, bf16[256,1536]{1,0:T(8,128)(2,1)S(1)}, u32[]{:S(2)}, u32[]{:S(2)}) collective-permute-start(bf16[256,1536]{1,0:T(8,128)(2,1)S(1)} %shard_map.127.refs_4_), channel_id=1, source_target_pairs={{0,8},{8,0},{16,24},{24,16},{1,9},{9,1},{17,25},{25,17},{2,10},{10... | collective-permute-start | bytes 2359304 | tf_op jit(solution)/shard_map/ppermute | solution.py:42
  35.5 15.2 %collective-permute-start.10 = (bf16[128,2048]{1,0:T(8,128)(2,1)}, bf16[128,2048]{1,0:T(8,128)(2,1)}, u32[]{:S(2)}, u32[]{:S(2)}) collective-permute-start(bf16[128,2048]{1,0:T(8,128)(2,1)} %collective-permute-done.1.refs_0_), channel_id=1, source_target_pairs={{0,2},{1,3},{2,0},{3,1},{4,6},{5,7},{6,4},{7,5},{8,10},{9,11},{10,... | collective-permute-start | bytes 1572872 | tf_op jit(solution)/shard_map/ppermute | solution.py:42
  37.1 24.8 %collective-permute-start.12 = (bf16[128,2048]{1,0:T(8,128)(2,1)S(1)}, bf16[128,2048]{1,0:T(8,128)(2,1)}, u32[]{:S(2)}, u32[]{:S(2)}) collective-permute-start(bf16[128,2048]{1,0:T(8,128)(2,1)S(1)} %collective-permute-done.2.refs_1_), channel_id=1, source_target_pairs={{0,2},{1,3},{2,0},{3,1},{4,6},{5,7},{6,4},{7,5},{8,10},{9,11},{10,... | collective-permute-start | bytes 1572872 | tf_op jit(solution)/shard_map/ppermute | solution.py:42
  37.5 24.4 %copy-start.30 = (bf16[128,2048]{1,0:T(8,128)(2,1)}, bf16[128,2048]{1,0:T(8,128)(2,1)S(1)}, u32[]{:S(2)}) copy-start(bf16[128,2048]{1,0:T(8,128)(2,1)S(1)} %collective-permute-done.6.refs_0_) | copy-start | bytes 1572868
  37.5 24.4 %copy-start.32 = (bf16[128,2048]{1,0:T(8,128)(2,1)}, bf16[128,2048]{1,0:T(8,128)(2,1)S(1)}, u32[]{:S(2)}) copy-start(bf16[128,2048]{1,0:T(8,128)(2,1)S(1)} %collective-permute-done.7.refs_1_) | copy-start | bytes 1572868
  40.8 39.7 %collective-permute-start.8 = (bf16[256,1536]{1,0:T(8,128)(2,1)}, bf16[256,1536]{1,0:T(8,128)(2,1)}, u32[]{:S(2)}, u32[]{:S(2)}) collective-permute-start(bf16[256,1536]{1,0:T(8,128)(2,1)} %shard_map.131.refs_0_), channel_id=1, source_target_pairs={{0,16},{8,24},{16,0},{24,8},{1,17},{9,25},{17,1},{25,9},{2,18},{10... | collective-permute-start | bytes 2359304 | tf_op jit(solution)/shard_map/ppermute | solution.py:42
  42.3 32.3 %collective-permute-start.11 = (bf16[128,2048]{1,0:T(8,128)(2,1)S(1)}, bf16[128,2048]{1,0:T(8,128)(2,1)}, u32[]{:S(2)}, u32[]{:S(2)}) collective-permute-start(bf16[128,2048]{1,0:T(8,128)(2,1)S(1)} %collective-permute-done.refs_1_), channel_id=1, source_target_pairs={{0,2},{1,3},{2,0},{3,1},{4,6},{5,7},{6,4},{7,5},{8,10},{9,11},{10,... | collective-permute-start | bytes 1572872 | tf_op jit(solution)/shard_map/ppermute | solution.py:42
  50.7 29.8 %collective-permute-start.5 = (bf16[128,2048]{1,0:T(8,128)(2,1)}, bf16[128,2048]{1,0:T(8,128)(2,1)}, u32[]{:S(2)}, u32[]{:S(2)}) collective-permute-start(bf16[128,2048]{1,0:T(8,128)(2,1)} %collective-permute-done.1.refs_0_), channel_id=1, source_target_pairs={{0,1},{1,0},{2,3},{3,2},{4,5},{5,4},{6,7},{7,6},{8,9},{9,8},{10,11... | collective-permute-start | bytes 1572872 | tf_op jit(solution)/shard_map/ppermute | solution.py:42
  61.9 26.4 %collective-permute-start.16 = (bf16[128,2048]{1,0:T(8,128)(2,1)}, bf16[128,2048]{1,0:T(8,128)(2,1)}, u32[]{:S(2)}, u32[]{:S(2)}) collective-permute-start(bf16[128,2048]{1,0:T(8,128)(2,1)} %collective-permute-done.10.refs_1_), channel_id=1, source_target_pairs={{0,1},{1,0},{2,3},{3,2},{4,5},{5,4},{6,7},{7,6},{8,9},{9,8},{10,11... | collective-permute-start | bytes 1572872 | tf_op jit(solution)/shard_map/ppermute | solution.py:42
  62.8 25.5 %collective-permute-start.17 = (bf16[128,2048]{1,0:T(8,128)(2,1)}, bf16[128,2048]{1,0:T(8,128)(2,1)}, u32[]{:S(2)}, u32[]{:S(2)}) collective-permute-start(bf16[128,2048]{1,0:T(8,128)(2,1)} %collective-permute-done.12.refs_1_), channel_id=1, source_target_pairs={{0,1},{1,0},{2,3},{3,2},{4,5},{5,4},{6,7},{7,6},{8,9},{9,8},{10,11... | collective-permute-start | bytes 1572872 | tf_op jit(solution)/shard_map/ppermute | solution.py:42
  79.0 19.8 %collective-permute-start.13 = (bf16[256,1536]{1,0:T(8,128)(2,1)}, bf16[256,1536]{1,0:T(8,128)(2,1)}, u32[]{:S(2)}, u32[]{:S(2)}) collective-permute-start(bf16[256,1536]{1,0:T(8,128)(2,1)} %shard_map.135), channel_id=1, source_target_pairs={{0,16},{8,24},{16,0},{24,8},{1,17},{9,25},{17,1},{25,9},{2,18},{10... | collective-permute-start | bytes 2359304 | tf_op jit(solution)/shard_map/ppermute | solution.py:42
  92.8 20.8 %collective-permute-start.18 = (bf16[256,1536]{1,0:T(8,128)(2,1)}, bf16[256,1536]{1,0:T(8,128)(2,1)}, u32[]{:S(2)}, u32[]{:S(2)}) collective-permute-start(bf16[256,1536]{1,0:T(8,128)(2,1)} %shard_map.139), channel_id=1, source_target_pairs={{0,8},{8,0},{16,24},{24,16},{1,9},{9,1},{17,25},{25,17},{2,10},{10... | collective-permute-start | bytes 2359304 | tf_op jit(solution)/shard_map/ppermute | solution.py:42
  93.4 41.3 %collective-permute-start.31 = (bf16[16,2048]{1,0:T(8,128)(2,1)}, bf16[16,2048]{1,0:T(8,128)(2,1)}, u32[]{:S(2)}, u32[]{:S(2)}) collective-permute-start(bf16[16,2048]{1,0:T(8,128)(2,1)} %bitcast.9), channel_id=1, source_target_pairs={{0,24},{8,16},{16,8},{24,0},{1,25},{9,17},{17,9},{25,1},{2,26},{10... | collective-permute-start | bytes 196616 | tf_op jit(solution)/shard_map/ppermute | solution.py:42
  94.9 16.9 %collective-permute-start.15 = (bf16[128,2048]{1,0:T(8,128)(2,1)}, bf16[128,2048]{1,0:T(8,128)(2,1)S(1)}, u32[]{:S(2)}, u32[]{:S(2)}) collective-permute-start(bf16[128,2048]{1,0:T(8,128)(2,1)} %collective-permute-done.11.refs_0_), channel_id=1, source_target_pairs={{0,1},{1,0},{2,3},{3,2},{4,5},{5,4},{6,7},{7,6},{8,9},{9,8},{10,11... | collective-permute-start | bytes 1572872 | tf_op jit(solution)/shard_map/ppermute | solution.py:42
  95.7 26.8 %collective-permute-start.24 = (bf16[128,1536]{1,0:T(8,128)(2,1)}, bf16[128,1536]{1,0:T(8,128)(2,1)}, u32[]{:S(2)}, u32[]{:S(2)}) collective-permute-start(bf16[128,1536]{1,0:T(8,128)(2,1)} %copy-done.39), channel_id=1, source_target_pairs={{0,16},{8,24},{16,0},{24,8},{1,17},{9,25},{17,1},{25,9},{2,18},{10... | collective-permute-start | bytes 1179656 | tf_op jit(solution)/shard_map/ppermute | solution.py:42
  98.8 24.7 %collective-permute-start.25 = (bf16[128,1536]{1,0:T(8,128)(2,1)}, bf16[128,1536]{1,0:T(8,128)(2,1)}, u32[]{:S(2)}, u32[]{:S(2)}) collective-permute-start(bf16[128,1536]{1,0:T(8,128)(2,1)} %copy-done.40), channel_id=1, source_target_pairs={{0,8},{8,0},{16,24},{24,16},{1,9},{9,1},{17,25},{25,17},{2,10},{10... | collective-permute-start | bytes 1179656 | tf_op jit(solution)/shard_map/ppermute | solution.py:42
  111.8 9.8 %copy-start.45 = (f32[3,16]{1,0:T(4,128)S(1)}, f32[3,16]{1,0:T(4,128)}, u32[]{:S(2)}) copy-start(f32[3,16]{1,0:T(4,128)} %param.23) | copy-start | bytes 580
  111.8 19.5 %collective-permute-start.26 = (bf16[128,1536]{1,0:T(8,128)(2,1)}, bf16[128,1536]{1,0:T(8,128)(2,1)}, u32[]{:S(2)}, u32[]{:S(2)}) collective-permute-start(bf16[128,1536]{1,0:T(8,128)(2,1)} %get-tuple-element.41), channel_id=1, source_target_pairs={{0,8},{8,0},{16,24},{24,16},{1,9},{9,1},{17,25},{25,17},{2,10},{10... | collective-permute-start | bytes 1179656 | tf_op jit(solution)/shard_map/ppermute | solution.py:42
  119.3 11.9 %collective-permute-start.27 = (bf16[128,1536]{1,0:T(8,128)(2,1)}, bf16[128,1536]{1,0:T(8,128)(2,1)}, u32[]{:S(2)}, u32[]{:S(2)}) collective-permute-start(bf16[128,1536]{1,0:T(8,128)(2,1)} %get-tuple-element.42), channel_id=1, source_target_pairs={{0,16},{8,24},{16,0},{24,8},{1,17},{9,25},{17,1},{25,9},{2,18},{10... | collective-permute-start | bytes 1179656 | tf_op jit(solution)/shard_map/ppermute | solution.py:42
  121.6 23.6 %copy-start.16 = (f32[128,1536]{1,0:T(8,128)S(1)}, f32[128,1536]{1,0:T(8,128)}, u32[]{:S(2)}) copy-start(f32[128,1536]{1,0:T(8,128)} %copy-done.15) | copy-start | bytes 2359300
  122.5 12.2 %collective-permute-start.30 = (bf16[16,2048]{1,0:T(8,128)(2,1)}, bf16[16,2048]{1,0:T(8,128)(2,1)S(1)}, u32[]{:S(2)}, u32[]{:S(2)}) collective-permute-start(bf16[16,2048]{1,0:T(8,128)(2,1)} %bitcast.9), channel_id=1, source_target_pairs={{0,16},{8,24},{16,0},{24,8},{1,17},{9,25},{17,1},{25,9},{2,18},{10... | collective-permute-start | bytes 196616 | tf_op jit(solution)/shard_map/ppermute | solution.py:42
  123.4 11.3 %collective-permute-start.29 = (bf16[16,2048]{1,0:T(8,128)(2,1)}, bf16[16,2048]{1,0:T(8,128)(2,1)S(1)}, u32[]{:S(2)}, u32[]{:S(2)}) collective-permute-start(bf16[16,2048]{1,0:T(8,128)(2,1)} %bitcast.9), channel_id=1, source_target_pairs={{0,8},{8,0},{16,24},{24,16},{1,9},{9,1},{17,25},{25,17},{2,10},{10... | collective-permute-start | bytes 196616 | tf_op jit(solution)/shard_map/ppermute | solution.py:42
  132.2 12.3 %collective-permute-start.28 = (bf16[3,1536]{1,0:T(4,128)(2,1)S(1)}, bf16[3,1536]{1,0:T(4,128)(2,1)S(1)}, u32[]{:S(2)}, u32[]{:S(2)}) collective-permute-start(bf16[3,1536]{1,0:T(4,128)(2,1)S(1)} %multiply_convert_fusion), channel_id=1, source_target_pairs={{0,8},{8,16},{16,24},{1,9},{9,17},{17,25},{2,10},{10,18},{18,26},{... | collective-permute-start | bytes 27656 | tf_op jit(solution)/shard_map/ppermute | solution.py:37
  153.1 37.2 %collective-permute-start.35 = (bf16[256,1024]{1,0:T(8,128)(2,1)}, bf16[256,1024]{1,0:T(8,128)(2,1)}, u32[]{:S(2)}, u32[]{:S(2)}) collective-permute-start(bf16[256,1024]{1,0:T(8,128)(2,1)} %get-tuple-element.48), channel_id=1, source_target_pairs={{0,8},{8,0},{16,24},{24,16},{1,9},{9,1},{17,25},{25,17},{2,10},{10... | collective-permute-start | bytes 1572872 | tf_op jit(solution)/shard_map/ppermute | solution.py:42
  154.6 10.1 %collective-permute-start.34 = (f32[16]{0:T(128)S(1)}, f32[16]{0:T(128)S(1)}, u32[]{:S(2)}, u32[]{:S(2)}) collective-permute-start(f32[16]{0:T(128)S(1)} %slice_reduce_fusion), channel_id=1, source_target_pairs={{0,24},{8,16},{16,8},{24,0},{1,25},{9,17},{17,9},{25,1},{2,26},{10... | collective-permute-start | bytes 200 | tf_op jit(solution)/shard_map/ppermute | solution.py:42
  155.0 9.7 %collective-permute-start.33 = (f32[16]{0:T(128)S(1)}, f32[16]{0:T(128)S(1)}, u32[]{:S(2)}, u32[]{:S(2)}) collective-permute-start(f32[16]{0:T(128)S(1)} %slice_reduce_fusion), channel_id=1, source_target_pairs={{0,16},{8,24},{16,0},{24,8},{1,17},{9,25},{17,1},{25,9},{2,18},{10... | collective-permute-start | bytes 200 | tf_op jit(solution)/shard_map/ppermute | solution.py:42
  156.7 8.4 %collective-permute-start.32 = (f32[16]{0:T(128)S(1)}, f32[16]{0:T(128)S(1)}, u32[]{:S(2)}, u32[]{:S(2)}) collective-permute-start(f32[16]{0:T(128)S(1)} %slice_reduce_fusion), channel_id=1, source_target_pairs={{0,8},{8,0},{16,24},{24,16},{1,9},{9,1},{17,25},{25,17},{2,10},{10... | collective-permute-start | bytes 200 | tf_op jit(solution)/shard_map/ppermute | solution.py:42
  173.2 27.6 %collective-permute-start.4 = (bf16[256,1024]{1,0:T(8,128)(2,1)}, bf16[256,1024]{1,0:T(8,128)(2,1)}, u32[]{:S(2)}, u32[]{:S(2)}) collective-permute-start(bf16[256,1024]{1,0:T(8,128)(2,1)} %shard_map.129), channel_id=1, source_target_pairs={{0,8},{8,0},{16,24},{24,16},{1,9},{9,1},{17,25},{25,17},{2,10},{10... | collective-permute-start | bytes 1572872 | tf_op jit(solution)/shard_map/ppermute | solution.py:42
  180.6 31.1 %collective-permute-start.9 = (bf16[256,1024]{1,0:T(8,128)(2,1)}, bf16[256,1024]{1,0:T(8,128)(2,1)}, u32[]{:S(2)}, u32[]{:S(2)}) collective-permute-start(bf16[256,1024]{1,0:T(8,128)(2,1)} %shard_map.133), channel_id=1, source_target_pairs={{0,16},{8,24},{16,0},{24,8},{1,17},{9,25},{17,1},{25,9},{2,18},{10... | collective-permute-start | bytes 1572872 | tf_op jit(solution)/shard_map/ppermute | solution.py:42
  185.5 31.7 %collective-permute-start.14 = (bf16[256,1024]{1,0:T(8,128)(2,1)}, bf16[256,1024]{1,0:T(8,128)(2,1)}, u32[]{:S(2)}, u32[]{:S(2)}) collective-permute-start(bf16[256,1024]{1,0:T(8,128)(2,1)} %shard_map.137), channel_id=1, source_target_pairs={{0,16},{8,24},{16,0},{24,8},{1,17},{9,25},{17,1},{25,9},{2,18},{10... | collective-permute-start | bytes 1572872 | tf_op jit(solution)/shard_map/ppermute | solution.py:42
  189.7 39.3 %collective-permute-start.19 = (bf16[256,1024]{1,0:T(8,128)(2,1)}, bf16[256,1024]{1,0:T(8,128)(2,1)S(1)}, u32[]{:S(2)}, u32[]{:S(2)}) collective-permute-start(bf16[256,1024]{1,0:T(8,128)(2,1)} %shard_map.141), channel_id=1, source_target_pairs={{0,8},{8,0},{16,24},{24,16},{1,9},{9,1},{17,25},{25,17},{2,10},{10... | collective-permute-start | bytes 1572872 | tf_op jit(solution)/shard_map/ppermute | solution.py:42
  192.6 44.5 %collective-permute-start.36 = (bf16[256,1024]{1,0:T(8,128)(2,1)}, bf16[256,1024]{1,0:T(8,128)(2,1)}, u32[]{:S(2)}, u32[]{:S(2)}) collective-permute-start(bf16[256,1024]{1,0:T(8,128)(2,1)} %fusion.1), channel_id=1, source_target_pairs={{0,16},{8,24},{1,17},{9,25},{2,18},{10,26},{3,19},{11,27},{4,20},{... | collective-permute-start | bytes 1572872 | tf_op jit(solution)/shard_map/ppermute | solution.py:37
  211.7 26.9 %collective-permute-start.20 = (bf16[128,1024]{1,0:T(8,128)(2,1)}, bf16[128,1024]{1,0:T(8,128)(2,1)S(1)}, u32[]{:S(2)}, u32[]{:S(2)}) collective-permute-start(bf16[128,1024]{1,0:T(8,128)(2,1)} %get-tuple-element.35), channel_id=1, source_target_pairs={{0,16},{8,24},{16,0},{24,8},{1,17},{9,25},{17,1},{25,9},{2,18},{10... | collective-permute-start | bytes 786440 | tf_op jit(solution)/shard_map/ppermute | solution.py:42
  215.7 13.3 %slice-start = ((s8[8388608]{0:T(1024)(128)(4,1)}), s8[4194304]{0:T(1024)(128)(4,1)S(1)}, s32[]{:S(2)}) async-start(s8[8388608]{0:T(1024)(128)(4,1)} %bitcast.46), calls=%async_computation | async-start | bytes 8388608
  215.7 13.3 %slice-start.1 = ((s8[8388608]{0:T(1024)(128)(4,1)}), s8[4194304]{0:T(1024)(128)(4,1)S(1)}, s32[]{:S(2)}) async-start(s8[8388608]{0:T(1024)(128)(4,1)} %bitcast.46), calls=%async_computation.1 | async-start | bytes 8388608
  215.7 22.9 %collective-permute-start.21 = (bf16[128,1024]{1,0:T(8,128)(2,1)}, bf16[128,1024]{1,0:T(8,128)(2,1)}, u32[]{:S(2)}, u32[]{:S(2)}) collective-permute-start(bf16[128,1024]{1,0:T(8,128)(2,1)} %get-tuple-element.36), channel_id=1, source_target_pairs={{0,8},{8,0},{16,24},{24,16},{1,9},{9,1},{17,25},{25,17},{2,10},{10... | collective-permute-start | bytes 786440 | tf_op jit(solution)/shard_map/ppermute | solution.py:42
  225.3 13.3 %collective-permute-start.22 = (bf16[128,1024]{1,0:T(8,128)(2,1)}, bf16[128,1024]{1,0:T(8,128)(2,1)S(1)}, u32[]{:S(2)}, u32[]{:S(2)}) collective-permute-start(bf16[128,1024]{1,0:T(8,128)(2,1)} %copy-done.41), channel_id=1, source_target_pairs={{0,8},{8,0},{16,24},{24,16},{1,9},{9,1},{17,25},{25,17},{2,10},{10... | collective-permute-start | bytes 786440 | tf_op jit(solution)/shard_map/ppermute | solution.py:42
  232.4 9.0 %copy-start.38 = (f32[1024]{0:T(1024)S(1)}, f32[1024]{0:T(1024)}, u32[]{:S(2)}) copy-start(f32[1024]{0:T(1024)} %param.25) | copy-start | bytes 12292
  232.4 12.8 %copy-start.1 = (f32[5,8,512]{2,1,0:T(8,128)S(1)}, f32[5,8,512]{2,1,0:T(8,128)}, u32[]{:S(2)}) copy-start(f32[5,8,512]{2,1,0:T(8,128)} %param.20) | copy-start | bytes 245764
  235.0 6.4 %collective-permute-start.23 = (bf16[128,1024]{1,0:T(8,128)(2,1)S(1)}, bf16[128,1024]{1,0:T(8,128)(2,1)S(1)}, u32[]{:S(2)}, u32[]{:S(2)}) collective-permute-start(bf16[128,1024]{1,0:T(8,128)(2,1)S(1)} %get-tuple-element.38), channel_id=1, source_target_pairs={{0,16},{8,24},{16,0},{24,8},{1,17},{9,25},{17,1},{25,9},{2,18},{10... | collective-permute-start | bytes 786440 | tf_op jit(solution)/shard_map/ppermute | solution.py:42
  (37 other events, 141.7 us)

commit v2 on v1

v2 whole, which is shorter than its diff:
```python
import functools
import jax
import jax.numpy as jnp
from jax import lax
from jax.experimental import pallas as pl
from jax.experimental.pallas import tpu as pltpu
from jax.sharding import PartitionSpec as P

H = 128
P_SIZE = 64
N = 256
G = 8
K = 4
SLOTS = 4
LANES = 128
EDGE = 8
LOG_ROWS = 16
LOG_PARTS = 3
EARLY = 2
TILE = 512
MIB = 1 << 20
VMEM_MIB = 58
SCALE = 64
BF16 = jnp.bfloat16
F32 = jnp.float32
VMEM = pl.BlockSpec(memory_space=pltpu.VMEM)
SMEM = pl.BlockSpec(memory_space=pltpu.SMEM)
ANY = pl.BlockSpec(memory_space=pl.ANY)


def shape_of(shape, dtype):
    return jax.ShapeDtypeStruct(shape, dtype)


def params():
    return pltpu.CompilerParams(vmem_limit_bytes=VMEM_MIB * MIB)


def cost(flops, moved, transcendentals=0):
    return pl.CostEstimate(
        flops=int(flops) // SCALE, bytes_accessed=int(moved) // SCALE, transcendentals=int(transcendentals) // SCALE
    )


def chained(values, after):
    return lax.optimization_barrier((*values, after))[: len(values)]


def passed_along(x, axis, by):
    length = lax.axis_size(axis)
    pairs = [(i, i + by) for i in range(length) if 0 <= i + by < length]
    return lax.ppermute(x, axis, pairs)


def swapped(x, axis, by):
    length = lax.axis_size(axis)
    return lax.ppermute(x, axis, [(i, i ^ by) for i in range(length)])


def pick_group(values, group_index, axis_index):
    return lax.dynamic_index_in_dim(values, group_index, axis_index, keepdims=False)


def dot32(a, b):
    return jnp.dot(a, b, preferred_element_type=F32)


def silu(v):
    return v / (1.0 + jnp.exp(-v))


def copy_all(pairs, sems):
    copies = [pltpu.make_async_copy(src, dst, sems.at[i]) for i, (src, dst) in enumerate(pairs)]
    for one in copies:
        one.start()
    for one in copies:
        one.wait()


def pack_kernel(place_ref, tok_ref, dt_ref, *refs):
    outs, sems = refs[:-1], refs[-1]
    local_heads, depth = dt_ref.shape
    part = outs[0].shape[0] - local_heads
    rows = pl.ds(pl.multiple_of(place_ref[0] * part, part), part)
    pairs = []
    for j, out in enumerate(outs, 1):
        cols = pl.ds(pl.multiple_of((place_ref[1] ^ j) * depth, depth), depth)
        pairs.append((tok_ref.at[rows, cols], out.at[:part]))
        pairs.append((dt_ref, out.at[part:]))
    copy_all(pairs, sems)


def pack(place, tokens, dt_t, n):
    local_heads, depth = dt_t.shape
    part = tokens.shape[0] // SLOTS
    return pl.pallas_call(
        pack_kernel,
        in_specs=[SMEM, ANY, ANY],
        out_specs=[ANY] * (n - 1),
        out_shape=[shape_of((part + local_heads, depth), BF16)] * (n - 1),
        scratch_shapes=[pltpu.SemaphoreType.DMA((2 * (n - 1),))],
        name="pack",
        compiler_params=params(),
    )(place, tokens, dt_t)


def join_kernel(part, count, *refs):
    blocks, out, sems = refs[:count], refs[-2], refs[-1]
    copy_all([(b.at[:part], out.at[i * part : (i + 1) * part]) for i, b in enumerate(blocks)], sems)


def join(blocks, part, after):
    depth = blocks[0].shape[1]
    return pl.pallas_call(
        functools.partial(join_kernel, part, len(blocks)),
        in_specs=[ANY] * (len(blocks) + len(after)),
        out_specs=ANY,
        out_shape=shape_of((part * len(blocks), depth), BF16),
        scratch_shapes=[pltpu.SemaphoreType.DMA((len(blocks),))],
        name="join",
        compiler_params=params(),
    )(*blocks, *after)


def sent_kernel(counts, main_tiles, *refs):
    total = sum(counts)
    rows, (w_ref, side_ref), outs = refs[:total], refs[total : total + 2], refs[-len(counts) :]
    tile = pl.program_id(0)

    def product(weights):
        x = jnp.concatenate([r[...] for r in rows], 0)
        result = dot32(x, weights[...]).astype(BF16)
        at = 0
        for out in outs:
            out[...] = result[at : at + out.shape[0]]
            at += out.shape[0]

    pl.when(tile < main_tiles)(lambda: product(w_ref))
    pl.when(tile >= main_tiles)(lambda: product(side_ref))


def weight_specs(depth, first_tile, main_tiles):
    return [
        pl.BlockSpec((depth, TILE), lambda i, *_: (0, first_tile + jnp.minimum(i, main_tiles - 1))),
        pl.BlockSpec((depth, TILE), lambda i, *_: (0, jnp.maximum(i - main_tiles, 0))),
    ]


def block_spec(part, depth, block):
    return pl.BlockSpec((part, depth), lambda i, *_: (block, 0))


def sent_product(name, part, rows, w_all, side, first_tile, tiles, after):
    depth = w_all.shape[0]
    main_tiles, total = tiles[0], sum(tiles)
    counts = [len(r) for r in rows]
    flat = [one for r in rows for one in r]
    return pl.pallas_call(
        functools.partial(sent_kernel, counts, main_tiles),
        grid=(total,),
        in_specs=[block_spec(part, depth, block) for _, block in flat]
        + weight_specs(depth, first_tile, main_tiles)
        + [ANY] * len(after),
        out_specs=[pl.BlockSpec((part * count, TILE), lambda i: (0, i)) for count in counts],
        out_shape=[shape_of((part * count, TILE * total), BF16) for count in counts],
        cost_estimate=cost(
            2 * part * len(flat) * depth * TILE * total, 2 * depth * (TILE * total + part * len(flat))
        ),
        name=name,
        compiler_params=params(),
    )(*[array for array, _ in flat], w_all, side, *after)


def kept_kernel(counts, main_tiles, stays, gones, place_ref, *refs):
    total, quarters = sum(counts), len(counts)
    rows, (w_ref, side_ref) = refs[:total], refs[total : total + 2]
    gots, outs = refs[total + 2 : total + 2 + quarters], refs[-2 * quarters :]
    tile = pl.program_id(0)
    part = rows[0].shape[0]

    def product(weights):
        x = jnp.concatenate([r[...] for r in rows], 0)
        result = dot32(x, weights[...])
        at = 0
        for q in range(quarters):
            whole = result[at : at + counts[q] * part] + gots[q][...].astype(F32)
            at += counts[q] * part
            for to, i in enumerate(stays[q]):
                outs[2 * q][to * part : (to + 1) * part] = whole[i * part : (i + 1) * part]
            for to, i in enumerate(gones[q]):
                outs[2 * q + 1][to * part : (to + 1) * part] = whole[i * part : (i + 1) * part].astype(BF16)

    pl.when(tile < main_tiles)(lambda: product(w_ref))
    pl.when(tile >= main_tiles)(lambda: product(side_ref))


def kept_product(name, part, place, tokens, rows, w_all, side, gots, first_tile, tiles, stays, gones, after):
    depth = w_all.shape[0]
    main_tiles, total = tiles[0], sum(tiles)
    counts = [len(r) + 1 for r in rows]
    arrays, specs, out_specs, out_shapes = [], [], [], []
    for q, quarter in enumerate(rows):
        arrays.append(tokens)
        specs.append(pl.BlockSpec((part, depth), lambda i, place, q=q: (place[1 + q], place[0])))
        for array, block in quarter:
            arrays.append(array)
            specs.append(block_spec(part, depth, block))
        for count, dtype in ((len(stays[q]), F32), (len(gones[q]), BF16)):
            out_specs.append(pl.BlockSpec((part * count, TILE), lambda i, place: (0, i)))
            out_shapes.append(shape_of((part * count, TILE * total), dtype))
    height = part * sum(counts)
    return pl.pallas_call(
        functools.partial(kept_kernel, counts, main_tiles, stays, gones),
        grid_spec=pltpu.PrefetchScalarGridSpec(
            num_scalar_prefetch=1,
            grid=(total,),
            in_specs=specs
            + weight_specs(depth, first_tile, main_tiles)
            + [pl.BlockSpec((part * count, TILE), lambda i, place: (0, i)) for count in counts]
            + [ANY] * len(after),
            out_specs=out_specs,
        ),
        out_shape=out_shapes,
        cost_estimate=cost(
            2 * height * depth * TILE * total, 2 * depth * (TILE * total + height) + 6 * height * TILE * total
        ),
        name=name,
        compiler_params=params(),
    )(place, *arrays, w_all, side, *gots, *after)


class Reduction:
    def __init__(self, name, part, quarters, first_tile, tiles, w_all, side):
        self.name, self.part, self.quarters = name, part, quarters
        self.first_tile, self.tiles = first_tile, tiles
        self.w_all, self.side = w_all, side
        self.n = len(quarters[0][1]) + 1

    def send(self, after):
        rows = [
            [blocks[j] for j in range(self.n) if j & order[0]] for _, blocks, order in self.quarters
        ]
        outs = sent_product(
            "sent_" + self.name, self.part, rows, self.w_all, self.side, self.first_tile, self.tiles, (after,)
        )
        self.gots = [swapped(out, "ctx", q[2][0]) for out, q in zip(outs, self.quarters)]
        return outs[0]

    def keep(self, slot, me, tokens, after):
        place = jnp.stack([me] + [slot ^ q[0] for q in self.quarters]).astype(jnp.int32)
        kept = [[j for j in range(self.n) if not j & order[0]] for _, _, order in self.quarters]
        gones = [[i for i, j in enumerate(k) if j & q[2][1]] for k, q in zip(kept, self.quarters)]
        stays = [[i for i, j in enumerate(k) if not j & q[2][1]] for k, q in zip(kept, self.quarters)]
        outs = kept_product(
            "kept_" + self.name,
            self.part,
            place,
            tokens,
            [[q[1][j] for j in k[1:]] for k, q in zip(kept, self.quarters)],
            self.w_all,
            self.side,
            self.gots,
            self.first_tile,
            self.tiles,
            stays,
            gones,
            (after,),
        )
        self.totals, self.lasts = [], []
        size = self.part
        for at, (k, stay, (_, _, order)) in enumerate(zip(kept, stays, self.quarters)):
            total, out = outs[2 * at : 2 * at + 2]
            k = [k[i] for i in stay]
            got = swapped(out, "ctx", order[1])
            for bit in order[2:]:
                total = total + got.astype(F32)
                gone = [i for i, j in enumerate(k) if j & bit]
                stay = [i for i, j in enumerate(k) if not j & bit]
                parts = [total[i * size : (i + 1) * size] for i in range(len(k))]
                out = jnp.concatenate([parts[i] for i in gone], 0).astype(BF16)
                total = jnp.concatenate([parts[i] for i in stay], 0)
                got = swapped(out, "ctx", bit)
                k = [k[i] for i in stay]
            self.totals.append(total)
            self.lasts.append(got)
        return outs[1]


def finished(total, last, scale):
    return ((total + last.astype(F32)) * scale).astype(BF16)


def finish_kernel(count, *refs):
    totals, lasts, scale_ref, outs = refs[:count], refs[count : 2 * count], refs[2 * count], refs[-count:]
    for total, last, out in zip(totals, lasts, outs):
        out[...] = finished(total[...], last[...], scale_ref[...])


def finish(name, totals, lasts, scale, after):
    count = len(totals)
    return pl.pallas_call(
        functools.partial(finish_kernel, count),
        in_specs=[VMEM] * (2 * count + 1) + [ANY] * len(after),
        out_specs=[VMEM] * count,
        out_shape=[shape_of(t.shape, BF16) for t in totals],
        cost_estimate=cost(4 * count * totals[0].size, 8 * count * totals[0].size),
        name=name,
        compiler_params=params(),
    )(*totals, *lasts, scale, *after)


def quarter_values(values, totals, lasts, scale):
    early = [v[...] for v in values]
    return early + [finished(t[...], l[...], scale) for t, l in zip(totals, lasts)]


def step_kernel(n, me_ref, tok_ref, *refs):
    weights, heads_ref = refs[:n], refs[n]
    shift_t_ref, cum_ref, fade_ref, log_ref, acc = refs[-5:]
    j = pl.program_id(0)

    @pl.when(j == 0)
    def _():
        acc[...] = jnp.zeros_like(acc)

    for i in range(n):

        @pl.when(j == i)
        def _():
            acc[...] += lax.dot_general(
                weights[i][...], tok_ref[...], (((1,), (1,)), ((), ())), preferred_element_type=F32
            )

    @pl.when(j == pl.num_programs(0) - 1)
    def _():
        v = acc[...] + heads_ref[:, 0:1]
        step = jnp.maximum(v, 0.0) + jnp.log1p(jnp.exp(-jnp.abs(v)))
        rate = -jnp.exp(heads_ref[:, 1:2]) * step
        rows = rate.shape[1]
        up_to = lax.broadcasted_iota(jnp.int32, (rows, rows), 0) <= lax.broadcasted_iota(
            jnp.int32, (rows, rows), 1
        )
        cum = jnp.dot(
            rate, up_to.astype(F32), precision=lax.Precision.HIGHEST, preferred_element_type=F32
        )
        last = cum[:, rows - 1 : rows]
        shift_t_ref[...] = cum - jnp.log(step)
        cum_ref[...] = cum.T
        fade_ref[...] = (jnp.exp(last - cum) * step).T
        log_ref[...] = jnp.broadcast_to(last.T, log_ref.shape)


def step_sizes(me, tokens, dt_t, payloads, heads, after):
    local_heads, depth = dt_t.shape
    n = len(payloads) + 1
    rows = tokens.shape[0]
    last = payloads[0].shape[0] // local_heads - 1
    whole = lambda shape: pl.BlockSpec(shape, lambda j, me: (0, 0))
    return pl.pallas_call(
        functools.partial(step_kernel, n),
        grid_spec=pltpu.PrefetchScalarGridSpec(
            num_scalar_prefetch=1,
            grid=(n,),
            in_specs=[
                pl.BlockSpec((rows, depth), lambda j, me: (0, me[0] ^ j)),
                whole((local_heads, depth)),
            ]
            + [pl.BlockSpec((local_heads, depth), lambda j, me: (last, 0))] * (n - 1)
            + [whole((local_heads, 3))]
            + [ANY] * len(after),
            out_specs=[
                whole((local_heads, rows)),
                whole((rows, local_heads)),
                whole((rows, local_heads)),
                whole((EDGE, local_heads)),
            ],
            scratch_shapes=[pltpu.VMEM((local_heads, rows), F32)],
        ),
        out_shape=[
            shape_of((local_heads, rows), F32),
            shape_of((rows, local_heads), F32),
            shape_of((rows, local_heads), F32),
            shape_of((EDGE, local_heads), F32),
        ],
        cost_estimate=cost(2 * n * rows * depth * LANES, 2 * n * rows * depth),
        name="steps",
        compiler_params=params(),
    )(me, tokens, dt_t, *payloads, heads, *after)


def write_logs(state_ref, parts):
    rows = lax.broadcasted_iota(jnp.int32, (LOG_ROWS, state_ref.shape[1]), 0)
    block = jnp.zeros((LOG_ROWS, state_ref.shape[1]), F32)
    for i, one in enumerate(parts):
        block = jnp.where(rows == i, one, block)
    state_ref[N:] = block.astype(BF16)


def read_logs(state_ref):
    block = state_ref[N:].astype(F32)
    return sum(block[i : i + 1] for i in range(LOG_PARTS))


def split_logs(logs):
    parts = []
    for _ in range(LOG_PARTS):
        parts.append(logs.astype(BF16).astype(F32))
        logs = logs - parts[-1]
    return parts


def head_spread(local_heads):
    channels = local_heads * P_SIZE
    hit = (
        lax.broadcasted_iota(jnp.int32, (local_heads, channels), 1) // P_SIZE
        == lax.broadcasted_iota(jnp.int32, (local_heads, channels), 0)
    )
    return hit.astype(F32).astype(BF16)


def spread_heads(values, hits):
    high = values.astype(BF16)
    low = (values - high.astype(F32)).astype(BF16)
    return dot32(high, hits) + dot32(low, hits)


def conv_kernel(place_ref, *refs):
    values, totals, lasts = refs[:EARLY], refs[EARLY:SLOTS], refs[SLOTS : 2 * SLOTS - EARLY]
    edge_ref, scale_ref, taps_ref, fade_ref, log_ref = refs[2 * SLOTS - EARLY : 2 * SLOTS - EARLY + 5]
    conv_ref, state_ref, vals = refs[-3:]
    part, width = totals[0].shape
    rows = part * SLOTS
    channels = width - 2 * N
    slot = place_ref[0]
    vals[:EDGE] = edge_ref[...]
    for k, value in enumerate(quarter_values(values, totals, lasts, scale_ref[...])):
        start = pl.multiple_of(EDGE + (slot ^ k) * part, EDGE)
        vals[pl.ds(start, part)] = value.astype(F32)
    for c in range(0, width, 2 * LANES):
        cols = slice(c, c + 2 * LANES)
        for r in range(0, rows, part):
            summed = taps_ref[K : K + 1, cols]
            for tap in range(K):
                at = r + EDGE - (K - 1) + tap
                summed = summed + taps_ref[tap : tap + 1, cols] * vals[at : at + part, cols]
            conv_ref[r : r + part, cols] = silu(summed).astype(BF16)
    hits = head_spread(channels // P_SIZE)
    faded = spread_heads(fade_ref[...], hits) * conv_ref[:, :channels].astype(F32)
    state_ref[:N] = lax.dot_general(
        conv_ref[:, channels : channels + N],
        faded.astype(BF16),
        (((0,), (0,)), ((), ())),
        preferred_element_type=F32,
    ).astype(BF16)
    left, parts = log_ref[...], []
    for _ in range(LOG_PARTS):
        parts.append(left.astype(BF16))
        left = left - parts[-1].astype(F32)
    spread = [dot32(one, hits)[0:1] for one in parts]
    write_logs(state_ref, spread)


def conv_and_state(slot, values, totals, lasts, edge, scale, taps, fade, logs, after):
    part, width = totals[0].shape
    rows = part * SLOTS
    return pl.pallas_call(
        conv_kernel,
        in_specs=[SMEM] + [VMEM] * (2 * SLOTS - EARLY + 5) + [ANY] * len(after),
        out_specs=[VMEM, VMEM],
        out_shape=[shape_of((rows, width), BF16), shape_of((N + LOG_ROWS, width - 2 * N), BF16)],
        scratch_shapes=[pltpu.VMEM((rows + EDGE, width), F32)],
        cost_estimate=cost(30 * rows * width, 12 * rows * width, 2 * rows * width),
        name="conv",
        compiler_params=params(),
    )(slot, *values, *totals, *lasts, edge, scale, taps, fade, logs, *after)


def inner_kernel(conv_ref, cum_ref, shift_t_ref, skip_ref, *refs):
    y_ref, scores = refs[-2:]
    rows, width = conv_ref.shape
    channels = width - 2 * N
    size = LANES
    blocks = rows // size
    nt = (((1,), (1,)), ((), ()))
    scores[...] = lax.dot_general(
        conv_ref[:, channels + N :], conv_ref[:, channels : channels + N], nt, preferred_element_type=F32
    )
    lower = lax.broadcasted_iota(jnp.int32, (size, size), 0) >= lax.broadcasted_iota(
        jnp.int32, (size, size), 1
    )
    left = lax.broadcasted_iota(jnp.int32, (size, 2 * P_SIZE), 1) < P_SIZE
    for pair in range(channels // (2 * P_SIZE)):
        cols = slice(pair * 2 * P_SIZE, (pair + 1) * 2 * P_SIZE)
        for a in range(blocks):
            t = slice(a * size, (a + 1) * size)
            products = []
            for h in (2 * pair, 2 * pair + 1):
                here = cum_ref[t, h : h + 1]
                own = jnp.where(lower, here - shift_t_ref[h : h + 1, t], -jnp.inf)
                weights = jnp.exp(own) * scores[t, t]
                if a > 0:
                    before = slice(0, a * size)
                    earlier = jnp.exp(here - shift_t_ref[h : h + 1, before]) * scores[t, before]
                    weights = jnp.concatenate([earlier, weights], 1)
                products.append(dot32(weights.astype(BF16), conv_ref[: (a + 1) * size, cols]))
            y_ref[t, cols] = jnp.where(left, products[0], products[1]) + skip_ref[:, cols] * conv_ref[
                t, cols
            ].astype(F32)


def inner_output(conved, cum, shift_t, skip, after):
    rows, width = conved.shape
    channels = width - 2 * N
    return pl.pallas_call(
        inner_kernel,
        in_specs=[VMEM] * 4 + [ANY] * len(after),
        out_specs=VMEM,
        out_shape=shape_of((rows, channels), F32),
        scratch_shapes=[pltpu.VMEM((rows, rows), F32)],
        cost_estimate=cost(2 * rows * rows * channels, 8 * rows * width, rows * rows * channels // P_SIZE),
        name="inner",
        compiler_params=params(),
    )(conved, cum, shift_t, skip, *after)


def merge_kernel(later_ref, own_ref, got_ref, *refs):
    out_ref = refs[-1]
    own_log, got_log = read_logs(own_ref), read_logs(got_ref)
    own, got = own_ref[:N].astype(F32), got_ref[:N].astype(F32)
    later = later_ref[0] > 0
    own_fall = jnp.where(later, 1.0, jnp.exp(got_log))
    got_fall = jnp.where(later, jnp.exp(own_log), 1.0)
    out_ref[:N] = (own_fall * own + got_fall * got).astype(BF16)
    write_logs(out_ref, split_logs(own_log + got_log))


def merged(later, own, got, after):
    return pl.pallas_call(
        merge_kernel,
        in_specs=[SMEM, VMEM, VMEM] + [ANY] * len(after),
        out_specs=VMEM,
        out_shape=shape_of(own.shape, BF16),
        cost_estimate=cost(4 * own.size, 6 * own.size),
        name="merge",
        compiler_params=params(),
    )(later, own, got, *after)


def final_kernel(whole_group, rounds, place_ref, *refs):
    values, totals, lasts = refs[:EARLY], refs[EARLY:SLOTS], refs[SLOTS : 2 * SLOTS - EARLY]
    refs = refs[2 * SLOTS - EARLY :]
    gots, refs = refs[:rounds], refs[rounds:]
    y_ref, conv_ref, init_ref, cum_ref, scale_ref, gain_ref = refs[:6]
    outs = refs[6:]
    part, channels = totals[0].shape
    slot = place_ref[0]
    hits = head_spread(channels // P_SIZE)
    state = jnp.zeros((N, channels), F32)
    log = jnp.zeros((1, channels), F32)
    for i, got in enumerate(gots):
        later = place_ref[1 + i] > 0
        state = state + jnp.where(later, jnp.exp(log), 0.0) * got[:N].astype(F32)
        log = log + jnp.where(later, read_logs(got), 0.0)
    state = state.astype(BF16)
    init = init_ref[...].astype(BF16)
    init_fall = jnp.exp(log)
    nt = (((1,), (1,)), ((), ()))
    for k, value in enumerate(quarter_values(values, totals, lasts, scale_ref[...])):
        at = pl.ds(pl.multiple_of((slot ^ k) * part, part), part)
        c_part = conv_ref[at, channels + N :]
        carried = dot32(c_part, state)
        carried = carried + init_fall * lax.dot_general(c_part, init, nt, preferred_element_type=F32)
        y = y_ref[at] + carried * spread_heads(jnp.exp(cum_ref[at]), hits)
        gated = y * silu(value.astype(F32))
        squares = jnp.sum(gated * gated, axis=1, keepdims=True)
        if whole_group:
            meansq = squares / (H // G * P_SIZE)
            outs[0][at] = (gated * lax.rsqrt(meansq + 1e-05) * gain_ref[...]).astype(BF16)
        else:
            outs[0][at] = gated
            outs[1][at] = jnp.broadcast_to(squares, (part, LANES))


def final_output(whole_group, place, values, totals, lasts, gots, y, conved, init, cum, scale, gain):
    rows, channels = y.shape
    if whole_group:
        outs = [shape_of((rows, channels), BF16)]
    else:
        outs = [shape_of((rows, channels), F32), shape_of((rows, LANES), F32)]
    return pl.pallas_call(
        functools.partial(final_kernel, whole_group, len(gots)),
        in_specs=[SMEM] + [VMEM] * (2 * SLOTS - EARLY + 6 + len(gots)),
        out_specs=[VMEM] * len(outs),
        out_shape=outs,
        cost_estimate=cost(2 * rows * channels * N, 12 * rows * channels, 2 * rows * channels),
        name="final",
        compiler_params=params(),
    )(place, *values, *totals, *lasts, *gots, y, conved, init, cum, scale, gain)


def body(
    tokens,
    w_zx,
    zx_scale,
    w_bc,
    bc_scale,
    w_dt,
    conv_x,
    conv_bc,
    tail_x,
    tail_bc,
    head_params,
    init_state,
    norm_gain,
):
    tok_rows = tokens.shape[0]
    depth = w_zx.shape[0]
    local_heads = head_params.shape[1]
    channels = local_heads * P_SIZE
    per_group = H // G
    n_ctx = lax.axis_size("ctx")
    me = lax.axis_index("ctx")
    head_place = lax.axis_index("head")
    group_index = head_place * local_heads // per_group
    bits = [1 << i for i in range(n_ctx.bit_length() - 1)]
    part = tok_rows // SLOTS
    slot = head_place % SLOTS
    slot_ref = slot[None].astype(jnp.int32)

    dt_t = w_dt.T
    payloads = pack(jnp.stack([slot, me]).astype(jnp.int32), tokens, dt_t, n_ctx)
    payloads = [swapped(one, "ctx", j) for j, one in enumerate(payloads, 1)]
    w_all = w_zx.reshape(depth, 2 * channels)
    bc_rows = pick_group(w_bc, group_index, 1)
    fetched = join(payloads, part, (w_all, bc_rows))
    from_chip = swapped(fetched, "head", 2)
    from_core = swapped(fetched, "head", 1)

    main = channels // TILE

    def quarter(k, rows):
        order = bits if k in (0, 3) else bits[::-1]
        return k, {j: (rows, j - 1) for j in range(1, n_ctx)}, order

    def first_of(*quarters):
        tiles = (main, 2 * N // TILE)
        name = "first" + "".join(str(q[0]) for q in quarters)
        return Reduction(name, part, quarters, main, tiles, w_all, bc_rows)

    def gate_of(*quarters):
        name = "gate" + "".join(str(q[0]) for q in quarters)
        return Reduction(name, part, quarters, 0, (main, 0), w_all, bc_rows)

    q0 = (0, {j: (one, 0) for j, one in enumerate(payloads, 1)}, bits)
    q1 = quarter(1, from_core)
    first0, first1, gate01 = first_of(q0), first_of(q1), gate_of(q0, q1)
    mark = first0.send(fetched)
    mark = first1.send(mark)
    mark = gate01.send(mark)
    shift_t, cum, fade, logs = step_sizes(
        me[None].astype(jnp.int32), tokens, dt_t, payloads, head_params.T, (mark,)
    )
    mark = first0.keep(slot, me, tokens, cum)
    mark = first1.keep(slot, me, tokens, mark)
    mark = gate01.keep(slot, me, tokens, mark)
    scale = jnp.concatenate([zx_scale[1], pick_group(bc_scale, group_index, 0)], 0)[None]
    firsts01 = finish(
        "fin_first", first0.totals + first1.totals, first0.lasts + first1.lasts, scale, (mark,)
    )
    mark = firsts01[0]
    from_both = swapped(chained([from_chip], mark)[0], "head", 1)
    q2, q3 = quarter(2, from_chip), quarter(3, from_both)
    first2, first3, gate23 = first_of(q2), first_of(q3), gate_of(q2, q3)
    mark = first2.send(mark)
    mark = first3.send(mark)
    gates01 = finish("fin_gate", gate01.totals, gate01.lasts, zx_scale[0:1], (mark,))
    mark = gates01[0]
    mark = first2.keep(slot, me, tokens, mark)
    mark = first3.keep(slot, me, tokens, mark)
    mark = gate23.send(mark)

    taps = jnp.concatenate([conv_x, pick_group(conv_bc, group_index, 1)], 1)
    edge = jnp.zeros((K - 1, scale.shape[1]), BF16)
    late = (first2, first3)
    for k in range(SLOTS):
        if k < EARLY:
            rows = firsts01[k][part - (K - 1) :]
        else:
            one = late[k - EARLY]
            rows = finished(one.totals[0][part - (K - 1) :], one.lasts[0][part - (K - 1) :], scale)
        edge = jnp.where((slot ^ k) == SLOTS - 1, rows, edge)
    arrived = passed_along(edge, "ctx", 1)
    previous = jnp.concatenate([tail_x, pick_group(tail_bc, group_index, 1)], 1)
    arrived = jnp.where(me == 0, previous, arrived).astype(F32)
    arrived = jnp.concatenate([jnp.zeros((EDGE - (K - 1), arrived.shape[1]), F32), arrived], 0)
    conved, local_state = conv_and_state(
        slot_ref, firsts01, first2.totals + first3.totals, first2.lasts + first3.lasts, arrived, scale, taps, fade, logs, (mark,)
    )
    mark = gate23.keep(slot, me, tokens, conved)
    y_local = inner_output(conved, cum, shift_t, jnp.repeat(head_params[2], P_SIZE)[None], (mark,))

    run, gots = local_state, []
    later = [((me & bit) > 0).astype(jnp.int32) for bit in bits]
    for i, bit in enumerate(bits):
        if bit == bits[-1]:
            gots.append(passed_along(run, "ctx", bit))
        else:
            gots.append(swapped(run, "ctx", bit))
            run = merged(later[i][None], run, gots[-1], (mark,))

    whole_group = local_heads >= per_group
    outs = final_output(
        whole_group,
        jnp.stack([slot.astype(jnp.int32)] + later),
        gates01,
        gate23.totals,
        gate23.lasts,
        gots,
        y_local,
        conved,
        init_state.reshape(channels, N),
        cum,
        zx_scale[0:1],
        norm_gain[None],
    )
    if whole_group:
        return outs[0]
    gated, squares = outs
    slot_hits = (jnp.arange(G) == group_index).astype(F32)
    group_sums = lax.psum(slot_hits[:, None] * squares[:, 0][None, :], "head")
    totals = lax.dynamic_index_in_dim(group_sums, group_index, 0, keepdims=False)
    meansq = totals / (per_group * P_SIZE)
    return (gated * lax.rsqrt(meansq + 1e-05)[:, None] * norm_gain).astype(BF16)


def solution(mesh):
    return jax.shard_map(
        body,
        mesh=mesh,
        in_specs=(
            P("ctx", None),
            P("ctx", None, "head"),
            P(None, "head"),
            P("ctx", None, None),
            P(),
            P("ctx", "head"),
            P(None, "head"),
            P(),
            P(None, "head"),
            P(),
            P(None, "head"),
            P("head", None, None),
            P("head"),
        ),
        out_specs=P("ctx", "head"),
        check_vma=False,
    )
```

time: 251 us -> 347 us (1.38); the launches traced: 246 us -> 346 us
  Pallas kernels: 78.5 us -> 213 us
  local copies, waits for them, and re-layouts: 76.2 us -> 37.1 us
  waiting for transfers between devices: 40.7 us -> 57.2 us
  starting transfers between devices: 41.7 us -> 30.8 us
    pallas_call x20 -> x21, Pallas kernels: 78.5 us -> 213 us  [the longest x1 55.4 us: pack(): pl.pallas_call(pack_kernel, in_specs=[SMEM, ANY, ANY], out_specs=[ANY] *...]
    unnamed x101 -> x67, local copies, waits for them, and re-layouts: 59.7 us -> 26.3 us
    ppermute x35 -> x23, waiting for transfers between devices: 40.7 us -> 57.2 us  [swapped(): return lax.ppermute(x, axis, [(i, i ^ by) for i in range(length)])]
    ppermute x35 -> x23, starting transfers between devices: 35.2 us -> 23.7 us  [swapped(): return lax.ppermute(x, axis, [(i, i ^ by) for i in range(length)])]
    convert_element_type x3 -> x0, other arithmetic: 4.74 us -> none  [the longest x1 2.29 us: body(): run = jnp.where(later, own_fall * got + run.astype(F32), got_fall * run.a...]
    another operation x5 -> x8, other arithmetic: 1.21 us -> 5.06 us  [the longest x6 3.77 us: keep(): jnp.stack([me] + [slot ^ q[0] for q in self.quarters]).astype(jnp.int32)]
  transfers between devices with their start and end apart: 37 -> 25, of which waited for: 11 -> 7; matrix products, arithmetic and copies ran while one was open for 13% -> 8% of each run, Pallas kernels for 28% -> 27%
where the time goes in v2:
time: 347 us; the launch traced here: 346 us
  Pallas kernels  213 us (61%)
  waiting for transfers between devices  57.2 us (16%)
  local copies, waits for them, and re-layouts  37.1 us (11%)
  starting transfers between devices  30.8 us (9%)
  other arithmetic  7.34 us (2%)
    ppermute x23, waiting for transfers between devices, swapped(): return lax.ppermute(x, axis, [(i, i ^ by) for i in range(length)])  57.2 us
    pallas_call x1, Pallas kernels, pack(): pl.pallas_call(pack_kernel, in_specs=[SMEM, ANY, ANY], out_specs=[ANY] *...  55.4 us
    pallas_call x1, Pallas kernels, join(): pl.pallas_call(functools.partial(join_kernel, part, len(blocks)), in_spec...  48.8 us
    pallas_call x6, Pallas kernels, kept_product(): pl.pallas_call(functools.partial(kept_kernel, counts, main_tiles, stays,...  40.7 us
    pallas_call x6, Pallas kernels, sent_product(): pl.pallas_call(functools.partial(sent_kernel, counts, main_tiles), grid=(...  34.3 us
    unnamed x67, local copies, waits for them, and re-layouts  26.3 us
    ppermute x23, starting transfers between devices, swapped(): return lax.ppermute(x, axis, [(i, i ^ by) for i in range(length)])  23.7 us
    dynamic_slice x4, local copies, waits for them, and re-layouts, pick_group(): lax.dynamic_index_in_dim(values, group_index, axis_index, keepdims=False)  8.86 us
  transfers between devices with their start and end apart: 25, of which 7 were waited for; matrix products, arithmetic and copies ran while one was open for 8% of the time, Pallas kernels for 27%

profile of v2, /device:TPU:0, one launch (start us, length us, event | category | flops | bytes accessed | tf_op | source)
XLA Modules:
  0.0 346.1 jit_solution(3606323349242669305)
XLA Ops:
  0.7 55.4 %pack.1 = (bf16[144,2048]{1,0:T(8,128)(2,1)}, bf16[144,2048]{1,0:T(8,128)(2,1)}, bf16[144,2048]{1,0:T(8,128)(2,1)}) custom-call(s32[2]{0:T(128)} %pad_add_fusion.2.place_ref, bf16[512,8192]{1,0:T(8,128)(2,1)} %refs_2_.3, bf16[16,2048]{1,0:T(8,128)(2,1)} %bitcast.54), custom_call_target="tpu_custom_call" | custom-call | tf_op jit(solution)/shard_map/pack/pallas_call | solution.py:96
  56.1 3.0 collective-permute-start
  59.1 1.5 collective-permute-start.1
  60.7 7.4 %constant_dynamic-slice_fusion.3 = bf16[2048,1,512]{2,1,0:T(2,128)(2,1)S(1)} fusion(bf16[2048,8,512]{2,1,0:T(8,128)(2,1)} %param.16, s32[]{:T(128)S(6)} %select_n.55), kind=kLoop, calls=%fused_computation.14 | loop fusion | bytes 4194308 | tf_op jit(solution)/shard_map/jit(dynamic_index_in_dim)/dynamic_slice | solution.py:61
  68.0 1.9 copy.25
  69.9 10.2 %copy.21 = bf16[256,8,2,1024]{3,1,2,0:T(8,128)(2,1)} copy(bf16[256,8,2,1024]{3,2,1,0:T(2,128)(2,1)} %bitcast.52) | data formatting | bytes 16777216
  80.2 6.4 %collective-permute-done.2.refs_2_.refs_1_.refs_3_ = bf16[144,2048]{1,0:T(8,128)(2,1)S(1)} collective-permute-done((bf16[144,2048]{1,0:T(8,128)(2,1)}, bf16[144,2048]{1,0:T(8,128)(2,1)S(1)}, u32[]{:S(2)}, u32[]{:S(2)}) %collective-permute-start.2) | collective-permute-done | bytes 589856 | tf_op jit(solution)/shard_map/ppermute | solution.py:57
  87.4 48.8 %join.1.refs_4_ = bf16[384,2048]{1,0:T(8,128)(2,1)} custom-call(bf16[144,2048]{1,0:T(8,128)(2,1)} %copy-done.5, bf16[144,2048]{1,0:T(8,128)(2,1)} %copy-done.4, bf16[144,2048]{1,0:T(8,128)(2,1)} %copy-done.6, bf16[2048,2048]{1,0:T(8,128)(2,1)} %bitcast.26, bf16[2048,512]{1,0:T(8,128)(2,1)} %bitcast.39), custom_call_target="tpu_custom_call" | custom-call | tf_op jit(solution)/shard_map/join/pallas_call | solution.py:114
  136.2 1.8 collective-permute-start.10
  138.0 5.4 %sent_first0.1.refs_4_ = bf16[256,1536]{1,0:T(8,128)(2,1)} custom-call(bf16[144,2048]{1,0:T(8,128)(2,1)} %copy-done.5, bf16[144,2048]{1,0:T(8,128)(2,1)} %copy-done.6, bf16[2048,2048]{1,0:T(8,128)(2,1)} %bitcast.27, bf16[2048,512]{1,0:T(8,128)(2,1)} %bitcast.40, bf16[384,2048]{1,0:T(8,128)(2,1)} %join.1.refs_4_), custom_call_target="tpu_custom_call" | custom-call | flops 25165824 | bytes 114688 | tf_op jit(solution)/shard_map/sent_first0/pallas_call | solution.py:158
  143.4 1.5 collective-permute-start.7
  144.9 1.1 copy-done.3
  146.1 5.4 %sent_first1.1.refs_6_ = bf16[256,1536]{1,0:T(8,128)(2,1)} custom-call(bf16[384,2048]{1,0:T(8,128)(2,1)} %copy-done.3, bf16[384,2048]{1,0:T(8,128)(2,1)} %copy-done.3, bf16[2048,2048]{1,0:T(8,128)(2,1)} %bitcast.28, bf16[2048,512]{1,0:T(8,128)(2,1)} %bitcast.41, bf16[256,1536]{1,0:T(8,128)(2,1)} %sent_first0.1.refs_4_), custom_call_target="tpu_custom_call" | custom-call | flops 25165824 | bytes 114688 | tf_op jit(solution)/shard_map/sent_first1/pallas_call | solution.py:158
  151.5 1.5 collective-permute-start.6
  154.9 6.2 %sent_gate01.1 = (bf16[256,1024]{1,0:T(8,128)(2,1)}, bf16[256,1024]{1,0:T(8,128)(2,1)}) custom-call(bf16[144,2048]{1,0:T(8,128)(2,1)} %copy-done.5, bf16[144,2048]{1,0:T(8,128)(2,1)} %copy-done.6, bf16[384,2048]{1,0:T(8,128)(2,1)} %copy-done.3, bf16[384,2048]{1,0:T(8,128)(2,1)} %copy-done.3, bf16[2048,2048]{1,0:T(8,128)(2,1)} %bitcast.29, ...), custom_call_target="tpu_custom_call" | custom-call | flops 33554432 | bytes 98304 | tf_op jit(solution)/shard_map/sent_gate01/pallas_call | solution.py:158
  162.2 7.0 %steps.1 = (f32[16,512]{1,0:T(8,128)}, f32[512,16]{1,0:T(8,128)}, f32[512,16]{1,0:T(8,128)}, f32[8,16]{1,0:T(8,128)}) custom-call(s32[1]{0:T(128)} %bitcast.3.me_ref, bf16[512,8192]{1,0:T(8,128)(2,1)} %refs_2_.3, bf16[16,2048]{1,0:T(8,128)(2,1)} %bitcast.55, bf16[144,2048]{1,0:T(8,128)(2,1)} %copy-done.5, bf16[144,2048]{1,0:T(8,128)(2,1)} %copy-done.4, ...), custom_call_target="tpu_custom_call" | custom-call | flops 16777216 | bytes 131072 | tf_op jit(solution)/shard_map/steps/pallas_call | solution.py:359
  170.1 6.5 %kept_first0.1 = (f32[128,1536]{1,0:T(8,128)}, bf16[128,1536]{1,0:T(8,128)(2,1)}) custom-call(s32[2]{0:T(128)} %pad_add_fusion.4.place_ref, bf16[512,8192]{1,0:T(8,128)(2,1)} %refs_2_.3, bf16[144,2048]{1,0:T(8,128)(2,1)} %copy-done.4, bf16[2048,2048]{1,0:T(8,128)(2,1)} %bitcast.30, bf16[2048,512]{1,0:T(8,128)(2,1)} %bitcast.43, ...), custom_call_target="tpu_custom_call" | custom-call | flops 25165824 | bytes 151552 | tf_op jit(solution)/shard_map/kept_first0/pallas_call | solution.py:212
  176.6 1.6 collective-permute-start.11
  179.0 6.7 %kept_first1.1 = (f32[128,1536]{1,0:T(8,128)}, bf16[128,1536]{1,0:T(8,128)(2,1)}) custom-call(s32[2]{0:T(128)} %pad_add_fusion.3.place_ref, bf16[512,8192]{1,0:T(8,128)(2,1)} %refs_2_.3, bf16[384,2048]{1,0:T(8,128)(2,1)} %copy-done.3, bf16[2048,2048]{1,0:T(8,128)(2,1)} %bitcast.31, bf16[2048,512]{1,0:T(8,128)(2,1)} %bitcast.44, bf16[256,1536]{1,0:T(8,128)(2,1)} %copy-done.9, ...), custom_call_target="tpu_custom_call" | custom-call | flops 25165824 | bytes 151552 | tf_op jit(solution)/shard_map/kept_first1/pallas_call | solution.py:212
  185.7 1.5 collective-permute-start.12
  191.4 7.2 %kept_gate01.1 = (f32[128,1024]{1,0:T(8,128)}, bf16[128,1024]{1,0:T(8,128)(2,1)}, f32[128,1024]{1,0:T(8,128)}, bf16[128,1024]{1,0:T(8,128)(2,1)}) custom-call(s32[3]{0:T(128)} %pad_add_fusion.1.place_ref, bf16[512,8192]{1,0:T(8,128)(2,1)} %refs_2_.3, bf16[144,2048]{1,0:T(8,128)(2,1)} %copy-done.4, bf16[512,8192]{1,0:T(8,128)(2,1)} %refs_2_.3, ...), custom_call_target="tpu_custom_call" | custom-call | flops 33554432 | bytes 147456 | tf_op jit(solution)/shard_map/kept_gate01/pallas_call | solution.py:212
  199.4 2.6 fin_first.1
  202.1 1.1 copy-done.1
  203.2 5.4 %sent_first2.1.refs_4_ = bf16[256,1536]{1,0:T(8,128)(2,1)} custom-call(bf16[384,2048]{1,0:T(8,128)(2,1)} %copy-done.1, bf16[384,2048]{1,0:T(8,128)(2,1)} %copy-done.1, bf16[2048,2048]{1,0:T(8,128)(2,1)} %bitcast.33, bf16[2048,512]{1,0:T(8,128)(2,1)} %bitcast.46, bf16[128,1536]{1,0:T(8,128)(2,1)} %get-tuple-element.53.refs_4_.refs_0_), custom_call_target="tpu_custom_call" | custom-call | flops 25165824 | bytes 114688 | tf_op jit(solution)/shard_map/sent_first2/pallas_call | solution.py:158
  209.1 1.2 copy-done.2
  210.3 5.4 %sent_first3.1.refs_5_ = bf16[256,1536]{1,0:T(8,128)(2,1)} custom-call(bf16[384,2048]{1,0:T(8,128)(2,1)} %copy-done.2, bf16[384,2048]{1,0:T(8,128)(2,1)} %copy-done.2, bf16[2048,2048]{1,0:T(8,128)(2,1)} %bitcast.34, bf16[2048,512]{1,0:T(8,128)(2,1)} %bitcast.47, bf16[256,1536]{1,0:T(8,128)(2,1)} %sent_first2.1.refs_4_), custom_call_target="tpu_custom_call" | custom-call | flops 25165824 | bytes 114688 | tf_op jit(solution)/shard_map/sent_first3/pallas_call | solution.py:158
  216.3 1.5 collective-permute-start.8
  217.8 1.5 collective-permute-start.9
  220.6 12.7 %collective-permute-done.8.refs_2_ = bf16[128,1024]{1,0:T(8,128)(2,1)S(1)} collective-permute-done((bf16[128,1024]{1,0:T(8,128)(2,1)S(1)}, bf16[128,1024]{1,0:T(8,128)(2,1)S(1)}, u32[]{:S(2)}, u32[]{:S(2)}) %collective-permute-start.8) | collective-permute-done | bytes 262176 | tf_op jit(solution)/shard_map/ppermute | solution.py:57
  233.3 6.9 %collective-permute-done.9.refs_3_ = bf16[128,1024]{1,0:T(8,128)(2,1)S(1)} collective-permute-done((bf16[128,1024]{1,0:T(8,128)(2,1)S(1)}, bf16[128,1024]{1,0:T(8,128)(2,1)S(1)}, u32[]{:S(2)}, u32[]{:S(2)}) %collective-permute-start.9) | collective-permute-done | bytes 262176 | tf_op jit(solution)/shard_map/ppermute | solution.py:57
  240.9 2.2 fin_gate.1
  244.0 6.6 %kept_first2.1 = (f32[128,1536]{1,0:T(8,128)}, bf16[128,1536]{1,0:T(8,128)(2,1)}) custom-call(s32[2]{0:T(128)} %pad_add_fusion.7.place_ref, bf16[512,8192]{1,0:T(8,128)(2,1)} %refs_2_.3, bf16[384,2048]{1,0:T(8,128)(2,1)} %copy-done.1, bf16[2048,2048]{1,0:T(8,128)(2,1)} %bitcast.35, bf16[2048,512]{1,0:T(8,128)(2,1)} %bitcast.48, ...), custom_call_target="tpu_custom_call" | custom-call | flops 25165824 | bytes 151552 | tf_op jit(solution)/shard_map/kept_first2/pallas_call | solution.py:212
  252.0 6.6 %kept_first3.1 = (f32[128,1536]{1,0:T(8,128)}, bf16[128,1536]{1,0:T(8,128)(2,1)}) custom-call(s32[2]{0:T(128)} %pad_add_fusion.6.place_ref, bf16[512,8192]{1,0:T(8,128)(2,1)} %refs_2_.3, bf16[384,2048]{1,0:T(8,128)(2,1)} %copy-done.2, bf16[2048,2048]{1,0:T(8,128)(2,1)} %bitcast.36, bf16[2048,512]{1,0:T(8,128)(2,1)} %bitcast.49, bf16[256,1536]{1,0:T(8,128)(2,1)} %copy-done.8, ...), custom_call_target="tpu_custom_call" | custom-call | flops 25165824 | bytes 151552 | tf_op jit(solution)/shard_map/kept_first3/pallas_call | solution.py:212
  258.5 1.5 collective-permute-start.19
  260.7 6.9 %collective-permute-done.19.refs_5_ = bf16[128,1536]{1,0:T(8,128)(2,1)S(1)} collective-permute-done((bf16[128,1536]{1,0:T(8,128)(2,1)}, bf16[128,1536]{1,0:T(8,128)(2,1)S(1)}, u32[]{:S(2)}, u32[]{:S(2)}) %collective-permute-start.19) | collective-permute-done | bytes 393248 | tf_op jit(solution)/shard_map/ppermute | solution.py:57
  268.7 3.4 collective-permute-start.20
  272.9 6.4 %sent_gate23.1 = (bf16[256,1024]{1,0:T(8,128)(2,1)}, bf16[256,1024]{1,0:T(8,128)(2,1)}) custom-call(bf16[384,2048]{1,0:T(8,128)(2,1)} %copy-done.1, bf16[384,2048]{1,0:T(8,128)(2,1)} %copy-done.1, bf16[384,2048]{1,0:T(8,128)(2,1)} %copy-done.2, bf16[384,2048]{1,0:T(8,128)(2,1)} %copy-done.2, bf16[2048,2048]{1,0:T(8,128)(2,1)} %bitcast.37, ...), custom_call_target="tpu_custom_call" | custom-call | flops 33554432 | bytes 98304 | tf_op jit(solution)/shard_map/sent_gate23/pallas_call | solution.py:158
  280.0 7.5 %conv.1 = (bf16[512,1536]{1,0:T(8,128)(2,1)}, bf16[272,1024]{1,0:T(8,128)(2,1)}) custom-call(s32[1]{0:T(128)} %bitcast.place_ref, bf16[128,1536]{1,0:T(8,128)(2,1)} %get-tuple-element.53.refs_4_.refs_0_, bf16[128,1536]{1,0:T(8,128)(2,1)} %get-tuple-element.61.refs_1_, f32[128,1536]{1,0:T(8,128)} %get-tuple-element.62.refs_2_, ...), custom_call_target="tpu_custom_call" | custom-call | flops 368640 | bytes 147456 | tf_op jit(solution)/shard_map/conv/pallas_call | solution.py:466
  287.5 1.5 collective-permute-start.23
  289.1 2.0 collective-permute-start.17
  291.7 7.7 %collective-permute-done.16.refs_6_ = bf16[256,1024]{1,0:T(8,128)(2,1)S(1)} collective-permute-done((bf16[256,1024]{1,0:T(8,128)(2,1)}, bf16[256,1024]{1,0:T(8,128)(2,1)S(1)}, u32[]{:S(2)}, u32[]{:S(2)}) %collective-permute-start.16) | collective-permute-done | bytes 524320 | tf_op jit(solution)/shard_map/ppermute | solution.py:57
  299.4 10.7 %collective-permute-done.17.refs_7_ = bf16[256,1024]{1,0:T(8,128)(2,1)S(1)} collective-permute-done((bf16[256,1024]{1,0:T(8,128)(2,1)}, bf16[256,1024]{1,0:T(8,128)(2,1)S(1)}, u32[]{:S(2)}, u32[]{:S(2)}) %collective-permute-start.17) | collective-permute-done | bytes 524320 | tf_op jit(solution)/shard_map/ppermute | solution.py:57
  311.0 7.2 %kept_gate23.1 = (f32[128,1024]{1,0:T(8,128)}, bf16[128,1024]{1,0:T(8,128)(2,1)}, f32[128,1024]{1,0:T(8,128)}, bf16[128,1024]{1,0:T(8,128)(2,1)}) custom-call(s32[3]{0:T(128)} %pad_add_fusion.5.place_ref, bf16[512,8192]{1,0:T(8,128)(2,1)} %refs_2_.3, bf16[384,2048]{1,0:T(8,128)(2,1)} %copy-done.1, bf16[512,8192]{1,0:T(8,128)(2,1)} %refs_2_.3, ...), custom_call_target="tpu_custom_call" | custom-call | flops 33554432 | bytes 147456 | tf_op jit(solution)/shard_map/kept_gate23/pallas_call | solution.py:212
  319.0 2.2 merge.1
  321.2 3.8 %collective-permute-start.24 = (bf16[272,1024]{1,0:T(8,128)(2,1)}, bf16[272,1024]{1,0:T(8,128)(2,1)S(1)}, u32[]{:S(2)}, u32[]{:S(2)}) collective-permute-start(bf16[272,1024]{1,0:T(8,128)(2,1)} %merge.1), channel_id=1, source_target_pairs={{0,16},{8,24},{1,17},{9,25},{2,18},{10,26},{3,19},{11,27},{4,20},{... | collective-permute-start | bytes 1671176 | tf_op jit(solution)/shard_map/ppermute | solution.py:52
  326.8 5.9 %inner.1.refs_8_ = f32[512,1024]{1,0:T(8,128)} custom-call(bf16[512,1536]{1,0:T(8,128)(2,1)} %get-tuple-element.66.refs_8_.conv_ref.refs_9_, f32[512,16]{1,0:T(8,128)} %get-tuple-element.44.refs_5_.cum_ref.refs_11_, f32[16,512]{1,0:T(8,128)} %get-tuple-element.72.shift_t_ref, f32[1,1024]{1,0:T(1,128)} %broadcast_in_dim_reshape.3.skip_ref, ...), custom_call_target="tpu_custom_call" | custom-call | flops 8388608 | bytes 98304 | tf_op jit(solution)/shard_map/inner/pallas_call | solution.py:514
  332.6 5.9 %collective-permute-done.22.refs_5_ = bf16[128,1024]{1,0:T(8,128)(2,1)S(1)} collective-permute-done((bf16[128,1024]{1,0:T(8,128)(2,1)}, bf16[128,1024]{1,0:T(8,128)(2,1)S(1)}, u32[]{:S(2)}, u32[]{:S(2)}) %collective-permute-start.22) | collective-permute-done | bytes 262176 | tf_op jit(solution)/shard_map/ppermute | solution.py:57
  339.4 6.7 %final.1 = bf16[512,1024]{1,0:T(8,128)(2,1)} custom-call(s32[3]{0:T(128)} %pad_add_fusion.place_ref, bf16[128,1024]{1,0:T(8,128)(2,1)} %get-tuple-element.55.refs_5_.refs_0_, bf16[128,1024]{1,0:T(8,128)(2,1)} %get-tuple-element.56.refs_1_, f32[128,1024]{1,0:T(8,128)} %get-tuple-element.67.refs_2_, f32[128,1024]{1,0:T(8,128)} %get-tuple-element.68.refs_3_, ...), custom_call_target="tpu_custom_call" | custom-call | flops 4194304 | bytes 98304 | tf_op jit(solution)/shard_map/final/pallas_call | solution.py:590
  (112 shorter events, 24.9 us)
Async XLA Ops:
  0.0 260.1 %copy-start = (f32[5,8,512]{2,1,0:T(8,128)S(1)}, f32[5,8,512]{2,1,0:T(8,128)}, u32[]{:S(2)}) copy-start(f32[5,8,512]{2,1,0:T(8,128)} %param.20) | copy-start | bytes 245764
  56.1 24.1 %collective-permute-start = (bf16[144,2048]{1,0:T(8,128)(2,1)}, bf16[144,2048]{1,0:T(8,128)(2,1)S(1)}, u32[]{:S(2)}, u32[]{:S(2)}) collective-permute-start(bf16[144,2048]{1,0:T(8,128)(2,1)} %get-tuple-element.39), channel_id=1, source_target_pairs={{0,16},{8,24},{16,0},{24,8},{1,17},{9,25},{17,1},{25,9},{2,18},{10... | collective-permute-start | bytes 1769480 | tf_op jit(solution)/shard_map/ppermute | solution.py:57
  59.1 21.0 %collective-permute-start.1 = (bf16[144,2048]{1,0:T(8,128)(2,1)}, bf16[144,2048]{1,0:T(8,128)(2,1)S(1)}, u32[]{:S(2)}, u32[]{:S(2)}) collective-permute-start(bf16[144,2048]{1,0:T(8,128)(2,1)} %get-tuple-element.40), channel_id=1, source_target_pairs={{0,8},{8,0},{16,24},{24,16},{1,9},{9,1},{17,25},{25,17},{2,10},{10... | collective-permute-start | bytes 1769480 | tf_op jit(solution)/shard_map/ppermute | solution.py:57
  60.6 25.9 %collective-permute-start.2 = (bf16[144,2048]{1,0:T(8,128)(2,1)}, bf16[144,2048]{1,0:T(8,128)(2,1)S(1)}, u32[]{:S(2)}, u32[]{:S(2)}) collective-permute-start(bf16[144,2048]{1,0:T(8,128)(2,1)} %get-tuple-element.41), channel_id=1, source_target_pairs={{0,24},{8,16},{16,8},{24,0},{1,25},{9,17},{17,9},{25,1},{2,26},{10... | collective-permute-start | bytes 1769480 | tf_op jit(solution)/shard_map/ppermute | solution.py:57
  80.2 6.4 %copy-start.4 = (bf16[144,2048]{1,0:T(8,128)(2,1)}, bf16[144,2048]{1,0:T(8,128)(2,1)S(1)}, u32[]{:S(2)}) copy-start(bf16[144,2048]{1,0:T(8,128)(2,1)S(1)} %collective-permute-done.refs_1_.refs_2_) | copy-start | bytes 1769476
  80.2 6.4 %copy-start.5 = (bf16[144,2048]{1,0:T(8,128)(2,1)}, bf16[144,2048]{1,0:T(8,128)(2,1)S(1)}, u32[]{:S(2)}) copy-start(bf16[144,2048]{1,0:T(8,128)(2,1)S(1)} %collective-permute-done.1.refs_0_.refs_1_) | copy-start | bytes 1769476
  136.2 8.8 %collective-permute-start.3 = (bf16[384,2048]{1,0:T(8,128)(2,1)}, bf16[384,2048]{1,0:T(8,128)(2,1)S(1)}, u32[]{:S(2)}, u32[]{:S(2)}) collective-permute-start(bf16[384,2048]{1,0:T(8,128)(2,1)} %join.1.refs_4_), channel_id=1, source_target_pairs={{0,1},{1,0},{2,3},{3,2},{4,5},{5,4},{6,7},{7,6},{8,9},{9,8},{10,11... | collective-permute-start | bytes 4718600 | tf_op jit(solution)/shard_map/ppermute | solution.py:57
  136.2 65.8 %collective-permute-start.10 = (bf16[384,2048]{1,0:T(8,128)(2,1)}, bf16[384,2048]{1,0:T(8,128)(2,1)S(1)}, u32[]{:S(2)}, u32[]{:S(2)}) collective-permute-start(bf16[384,2048]{1,0:T(8,128)(2,1)} %join.1.refs_4_), channel_id=1, source_target_pairs={{0,2},{1,3},{2,0},{3,1},{4,6},{5,7},{6,4},{7,5},{8,10},{9,11},{10,... | collective-permute-start | bytes 4718600 | tf_op jit(solution)/shard_map/ppermute | solution.py:57
  143.4 9.6 %copy-start.29 = (f32[3,16]{1,0:T(4,128)S(1)}, f32[3,16]{1,0:T(4,128)}, u32[]{:S(2)}) copy-start(f32[3,16]{1,0:T(4,128)} %param.23) | copy-start | bytes 580
  143.4 25.8 %collective-permute-start.7 = (bf16[256,1536]{1,0:T(8,128)(2,1)}, bf16[256,1536]{1,0:T(8,128)(2,1)S(1)}, u32[]{:S(2)}, u32[]{:S(2)}) collective-permute-start(bf16[256,1536]{1,0:T(8,128)(2,1)} %sent_first0.1.refs_4_), channel_id=1, source_target_pairs={{0,8},{8,0},{16,24},{24,16},{1,9},{9,1},{17,25},{25,17},{2,10},{10... | collective-permute-start | bytes 2359304 | tf_op jit(solution)/shard_map/ppermute | solution.py:57
  144.9 1.1 copy-start.3
  151.5 26.7 %collective-permute-start.6 = (bf16[256,1536]{1,0:T(8,128)(2,1)}, bf16[256,1536]{1,0:T(8,128)(2,1)S(1)}, u32[]{:S(2)}, u32[]{:S(2)}) collective-permute-start(bf16[256,1536]{1,0:T(8,128)(2,1)} %sent_first1.1.refs_6_), channel_id=1, source_target_pairs={{0,16},{8,24},{16,0},{24,8},{1,17},{9,25},{17,1},{25,9},{2,18},{10... | collective-permute-start | bytes 2359304 | tf_op jit(solution)/shard_map/ppermute | solution.py:57
  161.1 28.6 %collective-permute-start.4 = (bf16[256,1024]{1,0:T(8,128)(2,1)}, bf16[256,1024]{1,0:T(8,128)(2,1)S(1)}, u32[]{:S(2)}, u32[]{:S(2)}) collective-permute-start(bf16[256,1024]{1,0:T(8,128)(2,1)} %get-tuple-element.42.refs_5_), channel_id=1, source_target_pairs={{0,8},{8,0},{16,24},{24,16},{1,9},{9,1},{17,25},{25,17},{2,10},{10... | collective-permute-start | bytes 1572872 | tf_op jit(solution)/shard_map/ppermute | solution.py:57
  161.7 28.1 %collective-permute-start.5 = (bf16[256,1024]{1,0:T(8,128)(2,1)}, bf16[256,1024]{1,0:T(8,128)(2,1)S(1)}, u32[]{:S(2)}, u32[]{:S(2)}) collective-permute-start(bf16[256,1024]{1,0:T(8,128)(2,1)} %get-tuple-element.43), channel_id=1, source_target_pairs={{0,16},{8,24},{16,0},{24,8},{1,17},{9,25},{17,1},{25,9},{2,18},{10... | collective-permute-start | bytes 1572872 | tf_op jit(solution)/shard_map/ppermute | solution.py:57
  169.2 0.9 copy-start.11
  176.6 10.6 %copy-start.27 = (f32[2,1024]{1,0:T(2,128)S(1)}, f32[2,1024]{1,0:T(2,128)}, u32[]{:S(2)}) copy-start(f32[2,1024]{1,0:T(2,128)} %param.15) | copy-start | bytes 24580
  176.6 21.9 %collective-permute-start.11 = (bf16[128,1536]{1,0:T(8,128)(2,1)}, bf16[128,1536]{1,0:T(8,128)(2,1)S(1)}, u32[]{:S(2)}, u32[]{:S(2)}) collective-permute-start(bf16[128,1536]{1,0:T(8,128)(2,1)} %get-tuple-element.45.refs_5_), channel_id=1, source_target_pairs={{0,16},{8,24},{16,0},{24,8},{1,17},{9,25},{17,1},{25,9},{2,18},{10... | collective-permute-start | bytes 1179656 | tf_op jit(solution)/shard_map/ppermute | solution.py:57
  178.2 0.9 copy-start.9
  185.7 12.8 %collective-permute-start.12 = (bf16[128,1536]{1,0:T(8,128)(2,1)}, bf16[128,1536]{1,0:T(8,128)(2,1)S(1)}, u32[]{:S(2)}, u32[]{:S(2)}) collective-permute-start(bf16[128,1536]{1,0:T(8,128)(2,1)} %get-tuple-element.46.refs_8_), channel_id=1, source_target_pairs={{0,8},{8,0},{16,24},{24,16},{1,9},{9,1},{17,25},{25,17},{2,10},{10... | collective-permute-start | bytes 1179656 | tf_op jit(solution)/shard_map/ppermute | solution.py:57
  198.6 0.9 copy-start.20
  202.0 1.1 copy-start.1
  202.0 7.1 %collective-permute-start.13 = (bf16[384,2048]{1,0:T(8,128)(2,1)S(1)}, bf16[384,2048]{1,0:T(8,128)(2,1)S(1)}, u32[]{:S(2)}, u32[]{:S(2)}) collective-permute-start(bf16[384,2048]{1,0:T(8,128)(2,1)S(1)} %collective-permute-done.10.refs_0_.refs_1_), channel_id=1, source_target_pairs={{0,1},{1,0},{2,3},{3,2},{4,5},{5,4},{6,7},{7,6},{8,9},{9,8},{10,11... | collective-permute-start | bytes 4718600 | tf_op jit(solution)/shard_map/ppermute | solution.py:57
  208.6 7.7 %copy-start.21 = (bf16[128,1024]{1,0:T(8,128)(2,1)S(1)}, bf16[128,1024]{1,0:T(8,128)(2,1)}, u32[]{:S(2)}) copy-start(bf16[128,1024]{1,0:T(8,128)(2,1)} %get-tuple-element.49.refs_5_) | copy-start | bytes 786436
  208.6 9.3 %copy-start.30 = (bf16[128,1024]{1,0:T(8,128)(2,1)S(1)}, bf16[128,1024]{1,0:T(8,128)(2,1)}, u32[]{:S(2)}) copy-start(bf16[128,1024]{1,0:T(8,128)(2,1)} %get-tuple-element.50) | copy-start | bytes 786436
  208.6 34.5 %collective-permute-start.15 = (bf16[256,1536]{1,0:T(8,128)(2,1)}, bf16[256,1536]{1,0:T(8,128)(2,1)S(1)}, u32[]{:S(2)}, u32[]{:S(2)}) collective-permute-start(bf16[256,1536]{1,0:T(8,128)(2,1)} %sent_first2.1.refs_4_), channel_id=1, source_target_pairs={{0,16},{8,24},{16,0},{24,8},{1,17},{9,25},{17,1},{25,9},{2,18},{10... | collective-permute-start | bytes 2359304 | tf_op jit(solution)/shard_map/ppermute | solution.py:57
  209.1 1.2 copy-start.2
  215.8 35.3 %collective-permute-start.14 = (bf16[256,1536]{1,0:T(8,128)(2,1)}, bf16[256,1536]{1,0:T(8,128)(2,1)S(1)}, u32[]{:S(2)}, u32[]{:S(2)}) collective-permute-start(bf16[256,1536]{1,0:T(8,128)(2,1)} %sent_first3.1.refs_5_), channel_id=1, source_target_pairs={{0,8},{8,0},{16,24},{24,16},{1,9},{9,1},{17,25},{25,17},{2,10},{10... | collective-permute-start | bytes 2359304 | tf_op jit(solution)/shard_map/ppermute | solution.py:57
  216.3 17.0 %collective-permute-start.8 = (bf16[128,1024]{1,0:T(8,128)(2,1)S(1)}, bf16[128,1024]{1,0:T(8,128)(2,1)S(1)}, u32[]{:S(2)}, u32[]{:S(2)}) collective-permute-start(bf16[128,1024]{1,0:T(8,128)(2,1)S(1)} %copy-done.21), channel_id=1, source_target_pairs={{0,16},{8,24},{16,0},{24,8},{1,17},{9,25},{17,1},{25,9},{2,18},{10... | collective-permute-start | bytes 786440 | tf_op jit(solution)/shard_map/ppermute | solution.py:57
  217.8 22.3 %collective-permute-start.9 = (bf16[128,1024]{1,0:T(8,128)(2,1)S(1)}, bf16[128,1024]{1,0:T(8,128)(2,1)S(1)}, u32[]{:S(2)}, u32[]{:S(2)}) collective-permute-start(bf16[128,1024]{1,0:T(8,128)(2,1)S(1)} %copy-done.30), channel_id=1, source_target_pairs={{0,8},{8,0},{16,24},{24,16},{1,9},{9,1},{17,25},{25,17},{2,10},{10... | collective-permute-start | bytes 786440 | tf_op jit(solution)/shard_map/ppermute | solution.py:57
  233.3 6.9 %copy-start.24 = (bf16[128,1024]{1,0:T(8,128)(2,1)}, bf16[128,1024]{1,0:T(8,128)(2,1)S(1)}, u32[]{:S(2)}) copy-start(bf16[128,1024]{1,0:T(8,128)(2,1)S(1)} %collective-permute-done.8.refs_2_) | copy-start | bytes 786436
  243.1 0.9 copy-start.10
  250.5 9.6 %copy-start.26 = (f32[5,1024]{1,0:T(8,128)S(1)}, f32[5,1024]{1,0:T(8,128)}, u32[]{:S(2)}) copy-start(f32[5,1024]{1,0:T(8,128)} %param.19) | copy-start | bytes 61444
  250.5 10.2 %collective-permute-start.18 = (bf16[128,1536]{1,0:T(8,128)(2,1)}, bf16[128,1536]{1,0:T(8,128)(2,1)S(1)}, u32[]{:S(2)}, u32[]{:S(2)}) collective-permute-start(bf16[128,1536]{1,0:T(8,128)(2,1)} %get-tuple-element.57.refs_5_), channel_id=1, source_target_pairs={{0,8},{8,0},{16,24},{24,16},{1,9},{9,1},{17,25},{25,17},{2,10},{10... | collective-permute-start | bytes 1179656 | tf_op jit(solution)/shard_map/ppermute | solution.py:57
  251.1 0.9 copy-start.8
  258.5 9.1 %collective-permute-start.19 = (bf16[128,1536]{1,0:T(8,128)(2,1)}, bf16[128,1536]{1,0:T(8,128)(2,1)S(1)}, u32[]{:S(2)}, u32[]{:S(2)}) collective-permute-start(bf16[128,1536]{1,0:T(8,128)(2,1)} %get-tuple-element.58.refs_6_), channel_id=1, source_target_pairs={{0,16},{8,24},{16,0},{24,8},{1,17},{9,25},{17,1},{25,9},{2,18},{10... | collective-permute-start | bytes 1179656 | tf_op jit(solution)/shard_map/ppermute | solution.py:57
  260.7 18.6 %copy-start.17 = (bf16[128,1536]{1,0:T(8,128)(2,1)}, bf16[128,1536]{1,0:T(8,128)(2,1)S(1)}, u32[]{:S(2)}) copy-start(bf16[128,1536]{1,0:T(8,128)(2,1)S(1)} %collective-permute-done.18.refs_4_) | copy-start | bytes 1179652
  267.7 11.6 %copy-start.18 = (bf16[128,1536]{1,0:T(8,128)(2,1)}, bf16[128,1536]{1,0:T(8,128)(2,1)S(1)}, u32[]{:S(2)}) copy-start(bf16[128,1536]{1,0:T(8,128)(2,1)S(1)} %collective-permute-done.19.refs_5_) | copy-start | bytes 1179652
  268.7 10.6 %collective-permute-start.20 = (bf16[3,1536]{1,0:T(4,128)(2,1)S(1)}, bf16[3,1536]{1,0:T(4,128)(2,1)S(1)}, u32[]{:S(2)}, u32[]{:S(2)}) collective-permute-start(bf16[3,1536]{1,0:T(4,128)(2,1)S(1)} %fusion), channel_id=1, source_target_pairs={{0,8},{8,16},{16,24},{1,9},{9,17},{17,25},{2,10},{10,18},{18,26},{... | collective-permute-start | bytes 27656 | tf_op jit(solution)/shard_map/ppermute | solution.py:52
  272.9 6.5 %copy-start.28 = (bf16[3,1024]{1,0:T(4,128)(2,1)S(1)}, bf16[3,1024]{1,0:T(4,128)(2,1)}, u32[]{:S(2)}) copy-start(bf16[3,1024]{1,0:T(4,128)(2,1)} %param.21) | copy-start | bytes 18436
  287.5 30.7 %collective-permute-start.23 = (bf16[272,1024]{1,0:T(8,128)(2,1)}, bf16[272,1024]{1,0:T(8,128)(2,1)S(1)}, u32[]{:S(2)}, u32[]{:S(2)}) collective-permute-start(bf16[272,1024]{1,0:T(8,128)(2,1)} %get-tuple-element.71.own_ref), channel_id=1, source_target_pairs={{0,8},{8,0},{16,24},{24,16},{1,9},{9,1},{17,25},{25,17},{2,10},{10... | collective-permute-start | bytes 1671176 | tf_op jit(solution)/shard_map/ppermute | solution.py:57
  289.0 10.5 %collective-permute-start.16 = (bf16[256,1024]{1,0:T(8,128)(2,1)}, bf16[256,1024]{1,0:T(8,128)(2,1)S(1)}, u32[]{:S(2)}, u32[]{:S(2)}) collective-permute-start(bf16[256,1024]{1,0:T(8,128)(2,1)} %get-tuple-element.59.refs_11_), channel_id=1, source_target_pairs={{0,16},{8,24},{16,0},{24,8},{1,17},{9,25},{17,1},{25,9},{2,18},{10... | collective-permute-start | bytes 1572872 | tf_op jit(solution)/shard_map/ppermute | solution.py:57
  289.1 21.1 %collective-permute-start.17 = (bf16[256,1024]{1,0:T(8,128)(2,1)}, bf16[256,1024]{1,0:T(8,128)(2,1)S(1)}, u32[]{:S(2)}, u32[]{:S(2)}) collective-permute-start(bf16[256,1024]{1,0:T(8,128)(2,1)} %get-tuple-element.60), channel_id=1, source_target_pairs={{0,8},{8,0},{16,24},{24,16},{1,9},{9,1},{17,25},{25,17},{2,10},{10... | collective-permute-start | bytes 1572872 | tf_op jit(solution)/shard_map/ppermute | solution.py:57
  299.4 10.7 %copy-start.15 = (bf16[256,1024]{1,0:T(8,128)(2,1)}, bf16[256,1024]{1,0:T(8,128)(2,1)S(1)}, u32[]{:S(2)}) copy-start(bf16[256,1024]{1,0:T(8,128)(2,1)S(1)} %collective-permute-done.16.refs_6_) | copy-start | bytes 1572868
  321.2 17.3 %collective-permute-start.24 = (bf16[272,1024]{1,0:T(8,128)(2,1)}, bf16[272,1024]{1,0:T(8,128)(2,1)S(1)}, u32[]{:S(2)}, u32[]{:S(2)}) collective-permute-start(bf16[272,1024]{1,0:T(8,128)(2,1)} %merge.1), channel_id=1, source_target_pairs={{0,16},{8,24},{1,17},{9,25},{2,18},{10,26},{3,19},{11,27},{4,20},{... | collective-permute-start | bytes 1671176 | tf_op jit(solution)/shard_map/ppermute | solution.py:52
  325.0 7.6 %collective-permute-start.21 = (bf16[128,1024]{1,0:T(8,128)(2,1)}, bf16[128,1024]{1,0:T(8,128)(2,1)S(1)}, u32[]{:S(2)}, u32[]{:S(2)}) collective-permute-start(bf16[128,1024]{1,0:T(8,128)(2,1)} %get-tuple-element.69.refs_0_), channel_id=1, source_target_pairs={{0,8},{8,0},{16,24},{24,16},{1,9},{9,1},{17,25},{25,17},{2,10},{10... | collective-permute-start | bytes 786440 | tf_op jit(solution)/shard_map/ppermute | solution.py:57
  325.4 13.1 %collective-permute-start.22 = (bf16[128,1024]{1,0:T(8,128)(2,1)}, bf16[128,1024]{1,0:T(8,128)(2,1)S(1)}, u32[]{:S(2)}, u32[]{:S(2)}) collective-permute-start(bf16[128,1024]{1,0:T(8,128)(2,1)} %get-tuple-element.70), channel_id=1, source_target_pairs={{0,16},{8,24},{16,0},{24,8},{1,17},{9,25},{17,1},{25,9},{2,18},{10... | collective-permute-start | bytes 786440 | tf_op jit(solution)/shard_map/ppermute | solution.py:57
  332.6 5.9 %copy-start.22 = (bf16[128,1024]{1,0:T(8,128)(2,1)}, bf16[128,1024]{1,0:T(8,128)(2,1)S(1)}, u32[]{:S(2)}) copy-start(bf16[128,1024]{1,0:T(8,128)(2,1)S(1)} %collective-permute-done.21.refs_4_) | copy-start | bytes 786436
  338.5 0.9 copy-start.12
  (8 other events, 6.2 us)
